TPU v7x, 512 devices: a whole 4x8x8 slice. The times are simulated.
512 devices in a mesh: sec: 2 (over core), dp: 64 (over z, y), mp: 4 (over x).
Axes of the slice: x: 4, y: 8, z: 8, core: 2. Of those that a mesh axis runs over, the one named last changes fastest.
Arguments:
- patches: bfloat16 [32768, 1280], P(('sec', 'dp'), 'mp'), may hold values from -6 to 6
- window_index: int32 [32768], P(('sec', 'dp')), may hold values from 0 to 3, as said below
- vit_gain: bfloat16 [1280], replicated, may hold values from 0.25 to 1.75
- vit_qkv: bfloat16 [1280, 3, 640], P(None, None, 'mp'), may hold values from -0.15625 to 0.15625
- vit_proj: bfloat16 [640, 1280], P('mp'), may hold values from -0.25 to 0.25
- merge_gain: bfloat16 [1280], replicated, may hold values from 0.25 to 1.75
- piece_rows: int32 [8192], P(('sec', 'dp')), may hold values from 0 to 2, as said below
- piece_dest: int32 [8192], P(('sec', 'dp')), may hold values from 0 to 127, as said below
- visual_kv: bfloat16 [5120, 2, 512], P('mp'), may hold values from -0.078125 to 0.078125
- text_query: bfloat16 [32768, 4096], P(('sec', 'dp'), 'mp'), may hold values from -8 to 8
- text_kv: bfloat16 [32768, 2, 512], P(('sec', 'dp'), None, 'mp'), may hold values from -8 to 8
- out_cotangent: bfloat16 [32768, 4096], P(('sec', 'dp'), 'mp'), may hold values from -6 to 6
Outputs:
- attended: bfloat16 [32768, 4096], P(('sec', 'dp'), 'mp')
- visual_grad: bfloat16 [8192, 5120], P(('sec', 'dp'), 'mp')
Inputs may be any that keep to these rules, and one draw needn't show every extreme that they name: `window_index`: within each shard every window number names exactly 64 of its 256 patches. `piece_rows`: the 64 counts of a shard sum to 64; every shard has a piece of exactly 2 rows. `piece_dest`: the pieces of one shard go to distinct shards; in every draw some shard receives a piece of 2 rows from every shard.
All inputs are finite; a program needn't handle non-finite values.
Results may differ from a plain program's by a relative error of at most 0.02.
Values may be sent and summed in bfloat16 or wider, within the bound.
No kernel may reach another device: no remote copies, remote signals or barrier semaphores. Data moves between devices by JAX's collectives and lax.ppermute only.
A program may use at most 64 MiB of HBM per device.

v0:
```python
import math

import jax
import jax.numpy as jnp
from jax import lax
from jax.sharding import PartitionSpec as P

VIT_HD = 80
HD = 128


def rms_scale(values, gain):
    mean = jnp.mean(values * values, axis=-1, keepdims=True)
    return values * lax.rsqrt(mean + 1e-06) * gain


def attend(query, keys, values, allowed, cotangent):
    scale = 1.0 / math.sqrt(query.shape[-1])
    scores = jnp.einsum("ikgh,jkh->kgij", query, keys, preferred_element_type=jnp.float32) * scale
    scores = jnp.where(allowed[None, None], scores, -1e30)
    top = jnp.max(scores, axis=-1, keepdims=True)
    expo = jnp.exp(scores - top)
    probs = expo / jnp.sum(expo, axis=-1, keepdims=True)
    weights = probs.astype(jnp.bfloat16)
    output = jnp.einsum(
        "kgij,jkh->ikgh", weights, values, preferred_element_type=jnp.float32
    ).astype(jnp.bfloat16)
    dprobs = jnp.einsum("ikgh,jkh->kgij", cotangent, values, preferred_element_type=jnp.float32)
    delta = jnp.sum(probs * dprobs, axis=-1, keepdims=True)
    dscores = (probs * (dprobs - delta)).astype(jnp.bfloat16)
    dkeys = (
        jnp.einsum("kgij,ikgh->jkh", dscores, query, preferred_element_type=jnp.float32) * scale
    ).astype(jnp.bfloat16)
    dvalues = jnp.einsum(
        "kgij,ikgh->jkh", weights, cotangent, preferred_element_type=jnp.float32
    ).astype(jnp.bfloat16)
    return (output, dkeys, dvalues)


def send_out(data, flags):
    return (
        lax.all_to_all(data, ("sec", "dp"), split_axis=0, concat_axis=0, tiled=True),
        lax.all_to_all(flags, ("sec", "dp"), split_axis=0, concat_axis=0, tiled=True),
    )


def send_back(data):
    return lax.all_to_all(data, ("sec", "dp"), split_axis=0, concat_axis=0, tiled=True)


def project_kv(rows, visual_kv, position, merge):
    width_vit = rows.shape[1]
    kv_heads = visual_kv.shape[2] // HD
    kv_local = kv_heads // merge
    weight_heads = visual_kv.reshape(width_vit, 2, kv_heads, HD)
    term = jnp.einsum("sf,ftkd->kstd", rows, weight_heads, preferred_element_type=jnp.float32)
    summed_kv = lax.psum(term, "mp")
    own_kv = lax.dynamic_slice_in_dim(summed_kv, position * kv_local, kv_local, 0)
    return jnp.transpose(own_kv.astype(jnp.bfloat16), (1, 2, 0, 3))


def fold_heads(grads, visual_kv):
    return jnp.einsum(
        "std,ftd->sf",
        lax.all_gather(grads, "mp", axis=2, tiled=True),
        visual_kv,
        preferred_element_type=jnp.float32,
    )


def on_device(
    patches,
    window_index,
    vit_gain,
    vit_qkv,
    vit_proj,
    merge_gain,
    piece_rows,
    piece_dest,
    visual_kv,
    text_query,
    text_kv,
    out_cotangent,
):
    merge = lax.axis_size("mp")
    position = lax.axis_index("mp")
    sec_count = lax.axis_size("sec")
    dp_count = lax.axis_size("dp")
    shards = sec_count * dp_count
    whole = lax.all_gather(patches, "mp", axis=1, tiled=True)
    points, width_vit = whole.shape
    normed = rms_scale(whole.astype(jnp.float32), vit_gain.astype(jnp.float32)).astype(jnp.bfloat16)
    local_width = vit_qkv.shape[2]
    heads_here = local_width // VIT_HD
    qkv = jnp.dot(
        normed, vit_qkv.reshape(width_vit, 3 * local_width), preferred_element_type=jnp.float32
    )
    qkv = qkv.astype(jnp.bfloat16).reshape(points, 3, heads_here, VIT_HD)
    scores = jnp.einsum(
        "phd,qhd->hpq", qkv[:, 0], qkv[:, 1], preferred_element_type=jnp.float32
    ) / math.sqrt(VIT_HD)
    allowed = window_index[:, None] == window_index[None, :]
    scores = jnp.where(allowed[None], scores, -1e30)
    top = jnp.max(scores, axis=-1, keepdims=True)
    expo = jnp.exp(scores - top)
    weights = (expo / jnp.sum(expo, axis=-1, keepdims=True)).astype(jnp.bfloat16)
    mixed = jnp.einsum(
        "hpq,qhd->phd", weights, qkv[:, 2], preferred_element_type=jnp.float32
    ).astype(jnp.bfloat16)
    grouped = mixed.reshape(points // merge, merge, local_width)
    summed = lax.psum(
        jnp.einsum("mpc,cf->pmf", grouped, vit_proj, preferred_element_type=jnp.float32), "mp"
    )
    update = lax.dynamic_index_in_dim(summed, position, 0, keepdims=False)
    own_rows = lax.dynamic_index_in_dim(
        whole.reshape(points // merge, merge, width_vit), position, 1, keepdims=False
    )
    merged = rms_scale(
        own_rows.astype(jnp.float32) + update, merge_gain.astype(jnp.float32)
    ).astype(jnp.bfloat16)
    rows_here = merged.shape[0]
    pieces = piece_rows.shape[0]
    capacity = 2 * rows_here // pieces
    starts = jnp.cumsum(piece_rows) - piece_rows
    offsets = jnp.arange(capacity, dtype=jnp.int32)
    targets = jnp.arange(shards, dtype=jnp.int32)
    match = (piece_dest[None, :] == targets[:, None]).astype(jnp.int32)
    row_index = jnp.sum(
        match[:, :, None] * (starts[None, :, None] + offsets[None, None, :]), axis=1
    )
    inside = (offsets[None, None, :] < piece_rows[None, :, None]).astype(jnp.int32)
    live = jnp.sum(match[:, :, None] * inside, axis=1) > 0
    row_ids = jnp.arange(rows_here, dtype=jnp.int32)
    picker = ((row_index[:, :, None] == row_ids[None, None, :]) & live[:, :, None]).astype(
        jnp.bfloat16
    )
    picker = picker.reshape(shards * capacity, rows_here)
    flags = live.astype(jnp.bfloat16)
    slots = shards * capacity
    kv_local = visual_kv.shape[2] // HD // merge
    outgoing = jnp.dot(picker, merged, preferred_element_type=jnp.float32).astype(jnp.bfloat16)
    incoming, arrived = send_out(outgoing.reshape(shards, capacity, width_vit), flags)
    slot_kv = project_kv(incoming.reshape(slots, width_vit), visual_kv, position, merge)
    valid = arrived.reshape(slots) > 0.5
    text_rows = text_query.shape[0]
    group = text_query.shape[1] // (kv_local * HD)
    query = text_query.reshape(text_rows, kv_local, group, HD)
    cotangent = out_cotangent.reshape(text_rows, kv_local, group, HD)
    text_pairs = text_kv.reshape(text_rows, 2, kv_local, HD)
    keys = jnp.concatenate([slot_kv[:, 0], text_pairs[:, 0]], axis=0)
    values = jnp.concatenate([slot_kv[:, 1], text_pairs[:, 1]], axis=0)
    causal = jnp.arange(text_rows)[:, None] >= jnp.arange(text_rows)[None, :]
    visible = jnp.concatenate(
        [jnp.broadcast_to(valid[None, :], (text_rows, slots)), causal], axis=1
    )
    output, dkeys, dvalues = attend(query, keys, values, visible, cotangent)
    attended = output.reshape(text_rows, kv_local * group * HD)
    grads = jnp.stack([dkeys[:slots], dvalues[:slots]], axis=1).reshape(slots, 2, kv_local * HD)
    backward = (
        fold_heads(grads, visual_kv).astype(jnp.bfloat16).reshape(shards, capacity, width_vit)
    )
    returned = send_back(backward).reshape(slots, width_vit)
    visual_grad = jnp.einsum(
        "sr,sf->rf", picker, returned, preferred_element_type=jnp.float32
    ).astype(jnp.bfloat16)
    return (attended, visual_grad)


def solution(mesh):
    in_specs = (
        P(("sec", "dp"), "mp"),
        P(("sec", "dp")),
        P(),
        P(None, None, "mp"),
        P("mp", None),
        P(),
        P(("sec", "dp")),
        P(("sec", "dp")),
        P("mp", None, None),
        P(("sec", "dp"), "mp"),
        P(("sec", "dp"), None, "mp"),
        P(("sec", "dp"), "mp"),
    )
    out_specs = (P(("sec", "dp"), "mp"), P(("sec", "dp"), "mp"))
    return jax.shard_map(
        on_device, mesh=mesh, in_specs=in_specs, out_specs=out_specs, check_vma=False
    )
```

profile of v0, /device:TPU:1, one launch (start us, length us, event | category | flops | bytes accessed | tf_op | source)
XLA Modules:
  0.0 225.2 jit_solution(2808010435498009907)
XLA Ops:
  7.2 11.7 %all_gather.6 = bf16[256,1280]{0,1:T(8,128)(2,1)S(1)} all-gather(bf16[256,320]{0,1:T(8,128)(2,1)} %param.12), channel_id=1, replica_groups=mesh['sec'=2,'dp'=64,'mp'=4] {'mp'}, dimensions={1}, use_global_device_ids=true | all-gather | bytes 819200 | tf_op jit(solution)/shard_map/all_gather | solution.py:90
  19.1 0.7 convert_element_type.118
  19.8 0.9 broadcast_compare_fusion
  20.7 0.6 convolution_convert_fusion.1
  21.3 0.3 fusion.35
  21.6 0.4 fusion.102
  22.5 1.4 convolution_bitcast_fusion.1
  24.5 0.8 copy.98
  25.3 20.8 %all-to-all-start.1 = ((bf16[128,1,2]{2,1,0:T(2,128)(2,1)}), bf16[128,1,2]{2,1,0:T(2,128)(2,1)S(1)}, u32[]{:S(2)}, u32[]{:S(2)}) async-start(bf16[128,1,2]{2,1,0:T(2,128)(2,1)} %copy.98), calls=%async_computation.1 | async-start | bytes 131072 | tf_op jit(solution)/shard_map/all_to_all | solution.py:43
  47.1 0.3 dynamic-slice_convert_fusion
  47.4 41.7 %all-reduce.3.cloned.1.call-done = f32[4,64,1280]{2,1,0:T(8,128)} async-done(((f32[4,64,1280]{2,1,0:T(8,128)}), f32[4,64,1280]{2,1,0:T(8,128)}) %all-reduce.3.cloned.1.call-update) | async-done | bytes 1310736 | tf_op jit(solution)/shard_map/psum | solution.py:111
  89.1 1.1 multiply_reduce_fusion
  90.2 1.4 convolution_convert_fusion
  91.6 1.1 reshape.279
  92.7 15.9 %all-to-all-start = ((bf16[128,2,1280]{2,1,0:T(2,128)(2,1)}), bf16[128,2,1280]{2,1,0:T(2,128)(2,1)S(1)}, u32[]{:S(2)}, u32[]{:S(2)}) async-start(bf16[128,2,1280]{2,1,0:T(2,128)(2,1)} %reshape.279), calls=%async_computation | async-start | bytes 1310720 | tf_op jit(solution)/shard_map/all_to_all | solution.py:42
  108.6 5.3 %reshape.281 = bf16[1280,2,4,128]{3,2,1,0:T(4,128)(2,1)} reshape(bf16[1280,2,512]{2,1,0:T(2,128)(2,1)} %param.20) | data formatting | bytes 5242880 | tf_op jit(solution)/shard_map/reshape | solution.py:55
  114.6 17.2 %all-to-all-done = bf16[128,2,1280]{2,1,0:T(2,128)(2,1)S(1)} async-done(((bf16[128,2,1280]{2,1,0:T(2,128)(2,1)}), bf16[128,2,1280]{2,1,0:T(2,128)(2,1)S(1)}, u32[]{:S(2)}, u32[]{:S(2)}) %all-to-all-start) | async-done | bytes 655392 | tf_op jit(solution)/shard_map/all_to_all | solution.py:42
  132.1 2.6 %fusion.24 = f32[4,256,2,128]{3,1,0,2:T(8,128)S(1)} fusion(bf16[1280,2,4,128]{3,2,1,0:T(4,128)(2,1)} %reshape.281, bf16[256,1280,1,1]{1,0,2,3:T(8,128)(2,1)S(1)} %reshape.296), kind=kOutput, calls=%fused_computation.30 | convolution fusion | flops 671088640 | bytes 4325376 | tf_op jit(solution)/shard_map/sf,ftkd->kstd/dot_general | solution.py:56
  134.7 26.3 %all-reduce.4 = bf16[4,256,2,128]{3,1,0,2:T(8,128)(2,1)S(1)} all-reduce(f32[4,256,2,128]{3,1,0,2:T(8,128)S(1)} %fusion.24), channel_id=1, replica_groups=mesh['sec'=2,'dp'=64,'mp'=4] {'mp'}, use_global_device_ids=true, to_apply=%region_8.9 | all-reduce | flops 262144 | bytes 1572864 | tf_op jit(solution)/shard_map/psum | solution.py:57
  161.1 1.9 fusion.6
  163.0 0.9 fusion.5
  163.9 1.2 fusion.51
  165.1 1.5 fusion.1
  166.6 1.5 fusion.54
  168.1 9.7 %all-gather = bf16[256,2,1,512]{3,0,2,1:T(8,128)(2,1)S(1)} all-gather(bf16[256,2,1,128]{3,0,2,1:T(8,128)(2,1)S(1)} %pad_maximum_fusion), channel_id=2, replica_groups=mesh['sec'=2,'dp'=64,'mp'=4] {'mp'}, dimensions={3}, use_global_device_ids=true | all-gather | bytes 655360 | tf_op jit(solution)/shard_map/all_gather | solution.py:65
  177.8 0.9 fusion.10
  178.7 1.1 reshape.291
  179.8 14.4 %all-to-all-start.2 = ((bf16[128,2,1280]{2,1,0:T(2,128)(2,1)}), bf16[128,2,1280]{2,1,0:T(2,128)(2,1)S(1)}, u32[]{:S(2)}, u32[]{:S(2)}) async-start(bf16[128,2,1280]{2,1,0:T(2,128)(2,1)} %reshape.291), calls=%async_computation.2 | async-start | bytes 1310720 | tf_op jit(solution)/shard_map/all_to_all | solution.py:48
  194.2 3.5 %fusion.30 = bf16[128,8,256]{2,0,1:T(8,128)(2,1)S(1)} fusion(bf16[256,1,128]{2,0,1:T(8,128)(2,1)S(1)} %get-tuple-element.19, bf16[256,1,128]{2,0,1:T(8,128)(2,1)S(1)} %slice_bitcast_fusion.11, f32[8,256]{1,0:T(8,128)S(1)} %fusion.5, f32[8,256]{1,0:T(8,128)S(1)} %get-tuple-element.20, f32[512,256,8]{1,0,2:T(8,128)} %copy-done.1, ...), kind=kOutput, calls=%fused_computation.34 | convolution fusion | flops 274202624 | bytes 4997120 | tf_op jit(solution)/shard_map/kgij,jkh->ikgh/dot_general | solution.py:25
  197.7 1.0 copy.107
  198.7 18.7 %all-to-all-done.2 = bf16[128,2,1280]{2,1,0:T(2,128)(2,1)S(1)} async-done(((bf16[128,2,1280]{2,1,0:T(2,128)(2,1)}), bf16[128,2,1280]{2,1,0:T(2,128)(2,1)S(1)}, u32[]{:S(2)}, u32[]{:S(2)}) %all-to-all-start.2) | async-done | bytes 655392 | tf_op jit(solution)/shard_map/all_to_all | solution.py:48
  217.4 0.9 fusion.13
  (58 shorter events, 3.2 us)
Async XLA Ops:
  7.2 13.5 %copy-start = (bf16[1280,3,160]{0,2,1:T(8,128)(2,1)S(1)}, bf16[1280,3,160]{0,2,1:T(8,128)(2,1)}, u32[]{:S(2)}) copy-start(bf16[1280,3,160]{0,2,1:T(8,128)(2,1)} %param.15) | copy-start | bytes 3686404
  7.2 81.9 %all-reduce.3.cloned.1.call-start = ((), (), s32[]{:S(2)}) async-start(), calls=%async_computation.3 | async-start | bytes 2621440 | tf_op jit(solution)/shard_map/psum | solution.py:111
  18.9 3.6 %copy-start.4 = (bf16[160,1280]{1,0:T(8,128)(2,1)S(1)}, bf16[160,1280]{1,0:T(8,128)(2,1)}, u32[]{:S(2)}) copy-start(bf16[160,1280]{1,0:T(8,128)(2,1)} %param.16) | copy-start | bytes 1228804
  21.3 2.7 %copy-start.7 = (s32[64]{0:T(128)S(1)}, s32[64]{0:T(128)}, u32[]{:S(2)}) copy-start(s32[64]{0:T(128)} %param.18) | copy-start | bytes 772
  21.3 3.0 %copy-start.8 = (s32[64]{0:T(128)S(1)}, s32[64]{0:T(128)}, u32[]{:S(2)}) copy-start(s32[64]{0:T(128)} %param.19) | copy-start | bytes 772
  22.0 25.1 %copy-start.6 = (bf16[1280]{0:T(1024)(128)(2,1)S(1)}, bf16[1280]{0:T(1024)(128)(2,1)}, u32[]{:S(2)}) copy-start(bf16[1280]{0:T(1024)(128)(2,1)} %param.17) | copy-start | bytes 7684
  25.3 67.4 %all-to-all-start.1 = ((bf16[128,1,2]{2,1,0:T(2,128)(2,1)}), bf16[128,1,2]{2,1,0:T(2,128)(2,1)S(1)}, u32[]{:S(2)}, u32[]{:S(2)}) async-start(bf16[128,1,2]{2,1,0:T(2,128)(2,1)} %copy.98), calls=%async_computation.1 | async-start | bytes 131072 | tf_op jit(solution)/shard_map/all_to_all | solution.py:43
  91.6 22.3 %copy-start.5 = (bf16[256,2,128]{2,1,0:T(2,128)(2,1)S(1)}, bf16[256,2,128]{2,1,0:T(2,128)(2,1)}, u32[]{:S(2)}) copy-start(bf16[256,2,128]{2,1,0:T(2,128)(2,1)} %param.22) | copy-start | bytes 393220
  92.7 39.1 %all-to-all-start = ((bf16[128,2,1280]{2,1,0:T(2,128)(2,1)}), bf16[128,2,1280]{2,1,0:T(2,128)(2,1)S(1)}, u32[]{:S(2)}, u32[]{:S(2)}) async-start(bf16[128,2,1280]{2,1,0:T(2,128)(2,1)} %reshape.279), calls=%async_computation | async-start | bytes 1310720 | tf_op jit(solution)/shard_map/all_to_all | solution.py:42
  161.0 2.8 %copy-start.9 = (bf16[256,1024]{1,0:T(8,128)(2,1)S(1)}, bf16[256,1024]{1,0:T(8,128)(2,1)}, u32[]{:S(2)}) copy-start(bf16[256,1024]{1,0:T(8,128)(2,1)} %param.23) | copy-start | bytes 1572868
  163.0 3.6 %copy-start.1 = (f32[512,256,8]{1,0,2:T(8,128)}, f32[512,256,8]{1,0,2:T(8,128)S(1)}, u32[]{:S(2)}) copy-start(f32[512,256,8]{1,0,2:T(8,128)S(1)} %get-tuple-element.21) | copy-start | bytes 12582916
  165.1 1.5 copy-start.3
  166.6 11.2 %copy-start.2 = (bf16[1280,2,512]{2,1,0:T(2,128)(2,1)S(1)}, bf16[1280,2,512]{2,1,0:T(2,128)(2,1)}, u32[]{:S(2)}) copy-start(bf16[1280,2,512]{2,1,0:T(2,128)(2,1)} %param.20) | copy-start | bytes 7864324
  179.8 37.6 %all-to-all-start.2 = ((bf16[128,2,1280]{2,1,0:T(2,128)(2,1)}), bf16[128,2,1280]{2,1,0:T(2,128)(2,1)S(1)}, u32[]{:S(2)}, u32[]{:S(2)}) async-start(bf16[128,2,1280]{2,1,0:T(2,128)(2,1)} %reshape.291), calls=%async_computation.2 | async-start | bytes 1310720 | tf_op jit(solution)/shard_map/all_to_all | solution.py:48
Sparse Core Ops, SparseCore 0:
  24.1 64.9 all-reduce.2
where the time goes:
time: 226 us; the launch traced here: 225 us
  waiting for transfers between devices  77.7 us (34%)
  starting transfers between devices  51.1 us (23%)
  blocking collectives  47.7 us (21%)
  matrix products  18.2 us (8%)
  between operations  14.5 us (6%)
  local copies, waits for them, and re-layouts  11.2 us (5%)
  other arithmetic  4.88 us (2%)
    psum x1, waiting for transfers between devices, on_device(): lax.psum(jnp.einsum('mpc,cf->pmf', grouped, vit_proj, preferred_element_t...  41.7 us
    psum x1, blocking collectives, project_kv(): summed_kv = lax.psum(term, 'mp')  26.3 us
    all_to_all x1, starting transfers between devices, send_out(): lax.all_to_all(flags, ('sec', 'dp'), split_axis=0, concat_axis=0, tiled=T...  20.8 us
    all_to_all x1, waiting for transfers between devices, send_back(): lax.all_to_all(data, ('sec', 'dp'), split_axis=0, concat_axis=0, tiled=True)  18.7 us
    all_to_all x1, waiting for transfers between devices, send_out(): lax.all_to_all(data, ('sec', 'dp'), split_axis=0, concat_axis=0, tiled=True)  17.2 us
    all_to_all x1, starting transfers between devices, send_out(): lax.all_to_all(data, ('sec', 'dp'), split_axis=0, concat_axis=0, tiled=True)  15.9 us
    all_to_all x1, starting transfers between devices, send_back(): lax.all_to_all(data, ('sec', 'dp'), split_axis=0, concat_axis=0, tiled=True)  14.4 us
    all_gather x1, blocking collectives, on_device(): whole = lax.all_gather(patches, 'mp', axis=1, tiled=True)  11.7 us
  transfers between devices with their start and end apart: 4, of which 3 were waited for; matrix products, arithmetic and copies ran while one was open for 7% of the time, Pallas kernels for 0%

commit v1 on v0

v1 whole, which is shorter than its diff:
```python
import math

import jax
import jax.numpy as jnp
from jax import lax
from jax.experimental import pallas as pl
from jax.experimental.pallas import tpu as pltpu
from jax.sharding import PartitionSpec as P

VIT_HD = 80
HD = 128
EPS = 1e-6
NEG = -1e30
EMPTY = 2.0**100
LOG2E = math.log2(math.e)
F32 = jnp.float32
BF16 = jnp.bfloat16
VM = pl.BlockSpec(memory_space=pltpu.VMEM)
SM = pl.BlockSpec(memory_space=pltpu.SMEM)
TN = (((0,), (0,)), ((), ()))
NT = (((1,), (1,)), ((), ()))


def dot(a, b):
    return jnp.dot(a, b, preferred_element_type=F32)


def dotg(a, b, dims):
    return lax.dot_general(a, b, dims, preferred_element_type=F32)


def iota(shape, dim):
    return lax.broadcasted_iota(jnp.int32, shape, dim)


def call(kernel, out_shape, *args, flops=0, moved=0, limit=None, specs=None):
    return pl.pallas_call(
        kernel,
        out_shape=out_shape,
        in_specs=specs or [VM] * len(args),
        out_specs=jax.tree.map(lambda _: VM, out_shape),
        compiler_params=pltpu.CompilerParams(vmem_limit_bytes=limit or 16 * 2**20),
        cost_estimate=pl.CostEstimate(flops=flops, bytes_accessed=moved, transcendentals=0),
    )(*args)


def shape(dims, dtype=BF16):
    return jax.ShapeDtypeStruct(dims, dtype)


def prepare_kernel(
    wt_ref, gain_ref, win_ref, rows_ref, dest_ref, w_ref, bias_ref, pick_ref, pickt_ref, sent_ref
):
    w_ref[...] = (wt_ref[...].astype(F32) * gain_ref[...].astype(F32)).astype(BF16)
    wins = jnp.broadcast_to(win_ref[...].astype(F32), (256, 256))
    bias_ref[...] = jnp.where(wins == wins.T, 0.0, NEG)
    pieces = rows_ref.shape[1]
    a = iota((pieces, pieces), 0)
    b = iota((pieces, pieces), 1)
    rows = jnp.broadcast_to(rows_ref[...].astype(F32), (pieces, pieces))
    dest = jnp.broadcast_to(dest_ref[...].astype(F32), (pieces, pieces))
    starts = jnp.sum(jnp.where(b < a, rows, 0.0), axis=1, keepdims=True)
    count = jnp.sum(jnp.where(b == a, rows, 0.0), axis=1, keepdims=True)
    target = jnp.sum(jnp.where(b == a, dest, 0.0), axis=1, keepdims=True)
    lane = iota((pieces, 128), 1)
    row = (lane & 63).astype(F32)
    part = lane >> 6
    inside = (row >= starts) & (row < starts + count)
    code = jnp.sum(jnp.where(inside, target * 4.0 + row - starts, 0.0), axis=0, keepdims=True)
    code = code + 2.0 * part[:1].astype(F32)
    slots4 = pick_ref.shape[0]
    picks = jnp.where(iota((slots4, 128), 0).astype(F32) == code, 1.0, 0.0)
    pick_ref[...] = picks.astype(BF16)
    pickt_ref[...] = picks.T.astype(BF16)
    filled = jnp.sum(picks, axis=1, keepdims=True)
    key_row = (iota((slots4, 128), 0) & 2) == 0
    sent_ref[...] = jnp.where(key_row & (filled < 0.5), EMPTY, 0.0).astype(BF16)


def vit_kernel(pos_ref, x_ref, w_ref, bias_ref, proj_ref, part_ref, own_ref):
    x = x_ref[...]
    width, points = x.shape
    xf = x.astype(F32)
    scale = lax.rsqrt(jnp.sum(xf * xf, axis=0, keepdims=True) * (1.0 / width) + EPS)
    qkv = (dot(w_ref[...], x) * scale).astype(BF16)
    local = qkv.shape[0] // 3
    bias = bias_ref[...]
    mixed = []
    for h in range(local // VIT_HD):
        q = qkv[h * VIT_HD : (h + 1) * VIT_HD]
        k = qkv[local + h * VIT_HD : local + (h + 1) * VIT_HD]
        v = qkv[2 * local + h * VIT_HD : 2 * local + (h + 1) * VIT_HD]
        s = dotg(k, q, TN) * (LOG2E / math.sqrt(VIT_HD)) + bias
        e = jnp.exp2(s - jnp.max(s, axis=0, keepdims=True))
        weights = (e * (1.0 / jnp.sum(e, axis=0, keepdims=True))).astype(BF16)
        mixed.append(dot(v, weights).astype(BF16))
    mixed = jnp.concatenate(mixed, axis=0)
    n = iota((points, points), 1)
    perm = (iota((points, points), 0) == 4 * (n & 63) + (n >> 6)).astype(F32).astype(BF16)
    mixed = dot(mixed, perm).astype(BF16)
    part = dotg(mixed, proj_ref[...], TN).astype(BF16)
    for m in range(4):
        part_ref[m] = part[m * 64 : (m + 1) * 64]
    pos = pos_ref[0]
    sel = (iota((64, points), 1) == 4 * iota((64, points), 0) + pos).astype(F32).astype(BF16)
    own_ref[...] = dotg(sel, x, NT).astype(BF16)


def merge_kernel(in_ref, own_ref, gain_ref, w_ref, out_ref):
    resid = own_ref[...].astype(F32)
    for m in range(4):
        resid = resid + in_ref[m].astype(F32)
    scale = lax.rsqrt(jnp.mean(resid * resid, axis=1, keepdims=True) + EPS)
    merged = (resid * scale * gain_ref[...].astype(F32)).astype(BF16)
    kv = dot(merged, w_ref[...]).astype(BF16)
    for h in range(4):
        out_ref[h] = kv[:, h * 256 : (h + 1) * 256]


def pack_kernel(in_ref, pick_ref, sent_ref, out_ref):
    kv = in_ref[0].astype(F32)
    for m in range(1, 4):
        kv = kv + in_ref[m].astype(F32)
    kv = kv.astype(BF16)
    stack = jnp.concatenate([kv[:, :128], kv[:, 128:]], axis=0)
    out_ref[...] = (dot(pick_ref[...], stack) + sent_ref[...].astype(F32)).astype(BF16)


def text_kernel(
    q_ref, c_ref, k_ref, v_ref, qt_ref, ct_ref, ot_ref, m_ref, l_ref, d_ref, spread_ref, gather_ref
):
    rows = q_ref.shape[0]
    k = k_ref[...]
    v = v_ref[...]
    vt = v.T
    causal = iota((rows, rows), 0) <= iota((rows, rows), 1)
    for g in range(q_ref.shape[1] // HD):
        qt = q_ref[:, g * HD : (g + 1) * HD].T
        ct = c_ref[:, g * HD : (g + 1) * HD].T
        qt_ref[g] = qt
        ct_ref[g] = ct
        s = jnp.where(causal, dot(k, qt) * (LOG2E / math.sqrt(HD)), NEG)
        m = jnp.max(s, axis=0, keepdims=True)
        e = jnp.exp2(s - m)
        dp = dot(v, ct)
        m_ref[g : g + 1] = m
        l_ref[g : g + 1] = jnp.sum(e, axis=0, keepdims=True)
        d_ref[g : g + 1] = jnp.sum(e * dp, axis=0, keepdims=True)
        ot_ref[g] = dot(vt, e.astype(BF16))
    total = gather_ref.shape[0]
    half = total // 2
    a = iota((total, total), 0)
    b = iota((total, total), 1)

    def place(j):
        slot = j & (half - 1)
        return 4 * (slot >> 1) + 2 * (j >= half).astype(jnp.int32) + (slot & 1)

    gather_ref[...] = (b == place(a)).astype(F32).astype(BF16)
    spread_ref[...] = (a == place(b)).astype(F32).astype(BF16)


def slots_kernel(
    in_ref, gather_ref, spread_ref, q_ref, c_ref, qt_ref, ct_ref, m_ref, l_ref, d_ref,
    out_ref, w_ref, vt_ref, a_ref,
):
    slots = in_ref.shape[0] // 2
    kv = dot(gather_ref[...], in_ref[...])
    keys = kv[:slots]
    live = jnp.broadcast_to(keys[:, :1] < 0.5 * EMPTY, keys.shape)
    k = jnp.where(live, keys, 0.0).astype(BF16)
    v = kv[slots:].astype(BF16)
    vt_ref[...] = v.T
    bias = jnp.where(live, 0.0, NEG)
    bias = jnp.concatenate([bias, bias], axis=1)
    dk = jnp.zeros((slots, HD), F32)
    dv = jnp.zeros((slots, HD), F32)
    for g in range(qt_ref.shape[0]):
        s = dot(k, qt_ref[g]) * (LOG2E / math.sqrt(HD)) + bias
        dp = dot(v, ct_ref[g])
        mt = m_ref[g : g + 1]
        m = jnp.maximum(mt, jnp.max(s, axis=0, keepdims=True))
        e = jnp.exp2(s - m)
        alpha = jnp.exp2(mt - m)
        inv = 1.0 / (l_ref[g : g + 1] * alpha + jnp.sum(e, axis=0, keepdims=True))
        delta = (d_ref[g : g + 1] * alpha + jnp.sum(e * dp, axis=0, keepdims=True)) * inv
        a_ref[g : g + 1] = alpha * inv
        p = e * inv
        w = p.astype(BF16)
        ds = (p * (dp - delta)).astype(BF16)
        w_ref[g] = w
        dk = dk + dot(ds, q_ref[:, g * HD : (g + 1) * HD])
        dv = dv + dot(w, c_ref[:, g * HD : (g + 1) * HD])
    grads = jnp.concatenate([(dk * (1.0 / math.sqrt(HD))).astype(BF16), dv.astype(BF16)], axis=0)
    out_ref[...] = dot(spread_ref[...], grads).astype(BF16)


def output_kernel(ot_ref, a_ref, w_ref, vt_ref, out_ref):
    vt = vt_ref[...]
    for g in range(ot_ref.shape[0]):
        o = ot_ref[g] * a_ref[g : g + 1] + dot(vt, w_ref[g])
        out_ref[:, g * HD : (g + 1) * HD] = o.T.astype(BF16)


def rows_kernel(in_ref, pickt_ref, out_ref):
    g = dot(pickt_ref[...], in_ref[...]).astype(BF16)
    half = g.shape[0] // 2
    for m in range(4):
        out_ref[m, :, :HD] = g[:half]
        out_ref[m, :, HD:] = g[half:]


def fold_kernel(in_ref, w_ref, out_ref):
    grads = jnp.concatenate([in_ref[h] for h in range(4)], axis=1)
    out_ref[...] = dotg(grads, w_ref[...], NT).astype(BF16)


def exchange(x, axes):
    return lax.all_to_all(x, axes, split_axis=0, concat_axis=0, tiled=True)


def on_device(
    patches, window_index, vit_gain, vit_qkv, vit_proj, merge_gain, piece_rows, piece_dest,
    visual_kv, text_query, text_kv, out_cotangent,
):
    shards = lax.axis_size("sec") * lax.axis_size("dp")
    position = lax.axis_index("mp").astype(jnp.int32).reshape(1)
    points, width_part = patches.shape
    width = vit_qkv.shape[0]
    local = vit_qkv.shape[2]
    rows = text_query.shape[0]
    slots = 2 * shards
    merged_rows = points // 4

    gathered = exchange(jnp.broadcast_to(patches.T[None], (4, width_part, points)), "mp")
    x = gathered.reshape(width, points)
    wt = jnp.transpose(vit_qkv, (1, 2, 0)).reshape(3 * local, width)
    w_qkv, bias, pick, pickt, sent = call(
        prepare_kernel,
        (
            shape((3 * local, width)),
            shape((points, points), F32),
            shape((2 * slots, 128)),
            shape((128, 2 * slots)),
            shape((2 * slots, 128)),
        ),
        wt, vit_gain.reshape(1, width), window_index.reshape(1, points),
        piece_rows.reshape(1, -1), piece_dest.reshape(1, -1),
        flops=10**8, moved=3 * 10**6,
    )
    part, own = call(
        vit_kernel,
        (shape((4, merged_rows, width)), shape((merged_rows, width))),
        position, x, w_qkv, bias, vit_proj,
        specs=[SM] + [VM] * 4, flops=10**9, moved=4 * 10**6, limit=32 * 2**20,
    )
    summed = exchange(part, "mp")
    w_kv = jnp.transpose(visual_kv.reshape(width, 2, 4, HD), (0, 2, 1, 3)).reshape(width, 8 * HD)
    kv_part = call(
        merge_kernel, shape((4, merged_rows, 2 * HD)),
        summed, own, merge_gain.reshape(1, width), w_kv, flops=2 * 10**8, moved=4 * 10**6,
    )
    kv_terms = exchange(kv_part, "mp")
    outgoing = call(
        pack_kernel, shape((2 * slots, HD)), kv_terms, pick, sent, flops=2 * 10**7, moved=10**6,
    )
    incoming = exchange(outgoing.reshape(shards, 4, HD), ("sec", "dp")).reshape(2 * slots, HD)

    group = text_query.shape[1] // HD
    qt, ct, ot, top, total, delta, spread, gather = call(
        text_kernel,
        (
            shape((group, HD, rows)), shape((group, HD, rows)), shape((group, HD, rows), F32),
            shape((group, rows), F32), shape((group, rows), F32), shape((group, rows), F32),
            shape((2 * slots, 2 * slots)), shape((2 * slots, 2 * slots)),
        ),
        text_query, out_cotangent, text_kv[:, 0], text_kv[:, 1],
        flops=2 * 10**9, moved=5 * 10**6, limit=32 * 2**20,
    )
    grads, weights, vt, ratio = call(
        slots_kernel,
        (
            shape((2 * slots, HD)), shape((group, slots, rows)), shape((HD, slots)),
            shape((group, rows), F32),
        ),
        incoming, gather, spread, text_query, out_cotangent, qt, ct, top, total, delta,
        flops=2 * 10**9, moved=5 * 10**6, limit=32 * 2**20,
    )
    returned = exchange(grads.reshape(shards, 4, HD), ("sec", "dp")).reshape(2 * slots, HD)
    attended = call(
        output_kernel, shape((rows, group * HD)), ot, ratio, weights, vt,
        flops=2 * 10**9, moved=3 * 10**6, limit=32 * 2**20,
    )
    row_grads = call(
        rows_kernel, shape((4, merged_rows, 2 * HD)), returned, pickt, flops=2 * 10**7, moved=5 * 10**5,
    )
    heads = exchange(row_grads, "mp")
    visual_grad = call(
        fold_kernel, shape((merged_rows, width)), heads, w_kv, flops=2 * 10**8, moved=3 * 10**6,
    )
    return (attended, visual_grad)


def solution(mesh):
    both = ("sec", "dp")
    in_specs = (
        P(both, "mp"), P(both), P(), P(None, None, "mp"), P("mp", None), P(), P(both), P(both),
        P("mp", None, None), P(both, "mp"), P(both, None, "mp"), P(both, "mp"),
    )
    return jax.shard_map(
        on_device, mesh=mesh, in_specs=in_specs, out_specs=(P(both, "mp"), P(both, "mp")),
        check_vma=False,
    )
```

time: 226 us -> 125 us (0.55)
  waiting for transfers between devices: 77.7 us -> 14.5 us
  blocking collectives: 47.7 us -> 21.7 us
  local copies, waits for them, and re-layouts: 11.2 us -> 31.3 us
  matrix products: 18.2 us -> 0 us
  Pallas kernels: 0 us -> 15 us
  between operations: 14.5 us -> 0.79 us
  starting transfers between devices: 51.1 us -> 39.9 us
  other arithmetic: 4.88 us -> 0 us
    psum x1 -> x0, waiting for transfers between devices: 41.7 us -> none  [on_device(): lax.psum(jnp.einsum('mpc,cf->pmf', grouped, vit_proj, preferred_element_t...]
    psum x1 -> x0, blocking collectives: 26.3 us -> none  [project_kv(): summed_kv = lax.psum(term, 'mp')]
    unnamed x22 -> x60, local copies, waits for them, and re-layouts: 1.08 us -> 23.3 us
    all_to_all x0 -> x1, blocking collectives: none -> 21.7 us  [exchange(): return lax.all_to_all(x, axes, split_axis=0, concat_axis=0, tiled=True)]
    all_to_all x3 -> x5, waiting for transfers between devices: 36 us -> 14.5 us  [exchange(): return lax.all_to_all(x, axes, split_axis=0, concat_axis=0, tiled=True)]
    all_gather x2 -> x0, blocking collectives: 21.4 us -> none  [the longest x1 11.7 us: on_device(): whole = lax.all_gather(patches, 'mp', axis=1, tiled=True)]
    dot_general x13 -> x0, matrix products: 17.8 us -> none  [the longest x1 3.48 us: attend(): jnp.einsum('kgij,jkh->ikgh', weights, values, preferred_element_type=jnp....]
    pallas_call x0 -> x9, Pallas kernels: none -> 15 us  [call(): pl.pallas_call(kernel, out_shape=out_shape, in_specs=specs or [VM] * len(...]
  transfers between devices with their start and end apart: 4 -> 5, of which waited for: 3 -> 5; matrix products, arithmetic and copies ran while one was open for 7% -> 5% of each run, Pallas kernels for 0% -> 3%
where the time goes in v1:
time: 125 us; the launch traced here: 123 us
  starting transfers between devices  39.9 us (32%)
  local copies, waits for them, and re-layouts  31.3 us (25%)
  blocking collectives  21.7 us (17%)
  Pallas kernels  15 us (12%)
  waiting for transfers between devices  14.5 us (12%)
    all_to_all x5, starting transfers between devices, exchange(): return lax.all_to_all(x, axes, split_axis=0, concat_axis=0, tiled=True)  39.9 us
    unnamed x60, local copies, waits for them, and re-layouts  23.3 us
    all_to_all x1, blocking collectives, exchange(): return lax.all_to_all(x, axes, split_axis=0, concat_axis=0, tiled=True)  21.7 us
    pallas_call x9, Pallas kernels, call(): pl.pallas_call(kernel, out_shape=out_shape, in_specs=specs or [VM] * len(...  15 us
    all_to_all x5, waiting for transfers between devices, exchange(): return lax.all_to_all(x, axes, split_axis=0, concat_axis=0, tiled=True)  14.5 us
    reshape x1, local copies, waits for them, and re-layouts, on_device(): jnp.transpose(visual_kv.reshape(width, 2, 4, HD), (0, 2, 1, 3))  4.24 us
  transfers between devices with their start and end apart: 5, of which 5 were waited for; matrix products, arithmetic and copies ran while one was open for 5% of the time, Pallas kernels for 3%

profile of v1, /device:TPU:1, one launch (start us, length us, event | category | flops | bytes accessed | tf_op | source)
XLA Modules:
  0.0 123.3 jit_solution(10502238268575026643)
XLA Ops:
  0.6 1.9 %broadcast_in_dim.2 = bf16[4,320,256]{2,1,0:T(8,128)(2,1)} broadcast(bf16[320,256]{1,0:T(8,128)(2,1)} %bitcast.29), dimensions={1,2} | broadcast | bytes 819200 | tf_op jit(solution)/shard_map/broadcast_in_dim | solution.py:235
  2.5 4.8 %all-to-all-start = ((bf16[4,320,256]{2,1,0:T(8,128)(2,1)}), bf16[4,320,256]{2,1,0:T(8,128)(2,1)S(1)}, u32[]{:S(2)}, u32[]{:S(2)}) async-start(bf16[4,320,256]{2,1,0:T(8,128)(2,1)} %broadcast_in_dim.2), calls=%async_computation | async-start | bytes 1310720 | tf_op jit(solution)/shard_map/all_to_all | solution.py:219
  13.4 1.6 %all-to-all-done = bf16[4,320,256]{2,1,0:T(8,128)(2,1)S(1)} async-done(((bf16[4,320,256]{2,1,0:T(8,128)(2,1)}), bf16[4,320,256]{2,1,0:T(8,128)(2,1)S(1)}, u32[]{:S(2)}, u32[]{:S(2)}) %all-to-all-start) | async-done | bytes 655392 | tf_op jit(solution)/shard_map/all_to_all | solution.py:219
  15.0 1.0 copy-done.14
  17.0 3.0 %shard_map.133 = (bf16[4,64,1280]{2,1,0:T(8,128)(2,1)}, bf16[64,1280]{1,0:T(8,128)(2,1)S(1)}) custom-call(s32[1]{0:T(128)} %bitcast.2.pos_ref, bf16[1280,256]{1,0:T(8,128)(2,1)S(1)} %bitcast.21, bf16[480,1280]{1,0:T(8,128)(2,1)S(1)} %get-tuple-element.22.w_ref, f32[256,256]{1,0:T(8,128)S(1)} %copy-done.16, bf16[160,1280]{1,0:T(8,128)(2,1)S(1)} %copy-done.14), custom_call_target="tpu_custom_call" | custom-call | flops 1000000000 | bytes 4000000 | tf_op jit(solution)/shard_map/pallas_call | solution.py:37
  19.9 3.5 %all-to-all-start.1 = ((bf16[4,64,1280]{2,1,0:T(8,128)(2,1)}), bf16[4,64,1280]{2,1,0:T(8,128)(2,1)S(1)}, u32[]{:S(2)}, u32[]{:S(2)}) async-start(bf16[4,64,1280]{2,1,0:T(8,128)(2,1)} %get-tuple-element.24), calls=%async_computation.1 | async-start | bytes 1310720 | tf_op jit(solution)/shard_map/all_to_all | solution.py:219
  23.4 4.2 %reshape.56.w_ref = bf16[1280,1024]{1,0:T(8,128)(2,1)S(1)} reshape(bf16[1280,4,2,128]{3,2,1,0:T(2,128)(2,1)} %bitcast.28) | data formatting | bytes 5242880 | tf_op jit(solution)/shard_map/reshape | solution.py:258
  27.7 3.3 %all-to-all-done.1.in_ref = bf16[4,64,1280]{2,1,0:T(8,128)(2,1)S(1)} async-done(((bf16[4,64,1280]{2,1,0:T(8,128)(2,1)}), bf16[4,64,1280]{2,1,0:T(8,128)(2,1)S(1)}, u32[]{:S(2)}, u32[]{:S(2)}) %all-to-all-start.1) | async-done | bytes 655392 | tf_op jit(solution)/shard_map/all_to_all | solution.py:219
  31.0 1.4 %shard_map.134 = bf16[4,64,256]{2,1,0:T(8,128)(2,1)} custom-call(bf16[4,64,1280]{2,1,0:T(8,128)(2,1)S(1)} %all-to-all-done.1.in_ref, bf16[64,1280]{1,0:T(8,128)(2,1)S(1)} %get-tuple-element.25.own_ref, bf16[1,1280]{1,0:T(2,128)(2,1)S(1)} %reshape.54.gain_ref, bf16[1280,1024]{1,0:T(8,128)(2,1)S(1)} %reshape.56.w_ref), custom_call_target="tpu_custom_call" | custom-call | flops 200000000 | bytes 4000000 | tf_op jit(solution)/shard_map/pallas_call | solution.py:37
  32.4 3.3 %all-to-all-start.2 = ((bf16[4,64,256]{2,1,0:T(8,128)(2,1)}), bf16[4,64,256]{2,1,0:T(8,128)(2,1)S(1)}, u32[]{:S(2)}, u32[]{:S(2)}) async-start(bf16[4,64,256]{2,1,0:T(8,128)(2,1)} %shard_map.134), calls=%async_computation.2 | async-start | bytes 262144 | tf_op jit(solution)/shard_map/all_to_all | solution.py:219
  35.7 1.2 fusion
  36.9 3.6 %all-to-all-done.2.in_ref = bf16[4,64,256]{2,1,0:T(8,128)(2,1)S(1)} async-done(((bf16[4,64,256]{2,1,0:T(8,128)(2,1)}), bf16[4,64,256]{2,1,0:T(8,128)(2,1)S(1)}, u32[]{:S(2)}, u32[]{:S(2)}) %all-to-all-start.2) | async-done | bytes 131104 | tf_op jit(solution)/shard_map/all_to_all | solution.py:219
  43.2 24.9 %all-to-all-start.3 = ((bf16[128,4,128]{2,1,0:T(4,128)(2,1)}), bf16[128,4,128]{2,1,0:T(4,128)(2,1)S(1)}, u32[]{:S(2)}, u32[]{:S(2)}) async-start(bf16[128,4,128]{2,1,0:T(4,128)(2,1)} %bitcast.12), calls=%async_computation.3 | async-start | bytes 262144 | tf_op jit(solution)/shard_map/all_to_all | solution.py:219
  68.1 1.0 copy-done.10
  69.2 1.0 copy-done.12
  70.2 2.0 %shard_map.131 = (bf16[8,128,256]{2,1,0:T(8,128)(2,1)S(1)}, bf16[8,128,256]{2,1,0:T(8,128)(2,1)S(1)}, f32[8,128,256]{2,1,0:T(8,128)S(1)}, f32[8,256]{1,0:T(8,128...) custom-call(bf16[256,1024]{1,0:T(8,128)(2,1)S(1)} %copy-done.10, ...), custom_call_target="tpu_custom_call" | custom-call | flops 2000000000 | bytes 5000000 | tf_op jit(solution)/shard_map/pallas_call | solution.py:37
  72.2 1.0 copy-done.19
  76.4 4.8 %all-to-all-done.3 = bf16[128,4,128]{2,1,0:T(4,128)(2,1)S(1)} async-done(((bf16[128,4,128]{2,1,0:T(4,128)(2,1)}), bf16[128,4,128]{2,1,0:T(4,128)(2,1)S(1)}, u32[]{:S(2)}, u32[]{:S(2)}) %all-to-all-start.3) | async-done | bytes 131104 | tf_op jit(solution)/shard_map/all_to_all | solution.py:219
  81.3 1.0 copy-done.13
  82.3 1.0 copy-done.22
  83.3 1.0 copy-done.24
  84.4 1.0 copy-done.26
  85.4 1.0 copy-done.28
  86.5 3.6 %shard_map.136 = (bf16[512,128]{1,0:T(8,128)(2,1)S(1)}, bf16[8,256,256]{2,1,0:T(8,128)(2,1)S(1)}, bf16[128,256]{1,0:T(8,128)(2,1)S(1)}, f32[8,256]{1,0:T(8,128)S(1)}) custom-call(bf16[512,128]{1,0:T(8,128)(2,1)S(1)} %bitcast.23, bf16[512,512]{1,0:T(8,128)(2,1)S(1)} %copy-done.28, bf16[512,512]{1,0:T(8,128)(2,1)S(1)} %copy-done.26, ...), custom_call_target="tpu_custom_call" | custom-call | flops 2000000000 | bytes 5000000 | tf_op jit(solution)/shard_map/pallas_call | solution.py:37
  90.0 1.0 copy-done.17
  91.0 21.7 %all_to_all.30 = bf16[128,4,128]{2,1,0:T(4,128)(2,1)S(1)} all-to-all(bf16[128,4,128]{2,1,0:T(4,128)(2,1)S(1)} %bitcast.24), channel_id=1, replica_groups=mesh['sec'=2,'dp'=64,'mp'=4] {'sec','dp'}, dimensions={0} | all-to-all | bytes 262144 | tf_op jit(solution)/shard_map/all_to_all | solution.py:219
  113.6 3.3 %all-to-all-start.5 = ((bf16[4,64,256]{2,1,0:T(8,128)(2,1)}), bf16[4,64,256]{2,1,0:T(8,128)(2,1)S(1)}, u32[]{:S(2)}, u32[]{:S(2)}) async-start(bf16[4,64,256]{2,1,0:T(8,128)(2,1)} %shard_map.138), calls=%async_computation.5 | async-start | bytes 262144 | tf_op jit(solution)/shard_map/all_to_all | solution.py:219
  116.9 1.2 copy-done.18
  118.2 1.2 copy-done.20
  119.4 1.2 shard_map.137
  120.6 1.2 all-to-all-done.5.in_ref
  121.7 1.6 %shard_map.139 = bf16[64,1280]{1,0:T(8,128)(2,1)} custom-call(bf16[4,64,256]{2,1,0:T(8,128)(2,1)S(1)} %all-to-all-done.5.in_ref, bf16[1280,1024]{1,0:T(8,128)(2,1)S(1)} %reshape.56.w_ref), custom_call_target="tpu_custom_call" | custom-call | flops 200000000 | bytes 3000000 | tf_op jit(solution)/shard_map/pallas_call | solution.py:37
  (54 shorter events, 13.7 us)
Async XLA Ops:
  0.6 7.4 %copy-start = (bf16[1280,3,160]{0,2,1:T(8,128)(2,1)S(1)}, bf16[1280,3,160]{0,2,1:T(8,128)(2,1)}, u32[]{:S(2)}) copy-start(bf16[1280,3,160]{0,2,1:T(8,128)(2,1)} %param.15) | copy-start | bytes 3686404
  2.5 12.5 %all-to-all-start = ((bf16[4,320,256]{2,1,0:T(8,128)(2,1)}), bf16[4,320,256]{2,1,0:T(8,128)(2,1)S(1)}, u32[]{:S(2)}, u32[]{:S(2)}) async-start(bf16[4,320,256]{2,1,0:T(8,128)(2,1)} %broadcast_in_dim.2), calls=%async_computation | async-start | bytes 1310720 | tf_op jit(solution)/shard_map/all_to_all | solution.py:219
  8.1 0.7 copy-start.7
  8.7 0.7 copy-start.8
  9.4 0.7 copy-start.9
  12.7 0.7 copy-start.15
  13.4 10.0 %copy-start.29 = (bf16[1280]{0:T(1024)(128)(2,1)S(1)}, bf16[1280]{0:T(1024)(128)(2,1)}, u32[]{:S(2)}) copy-start(bf16[1280]{0:T(1024)(128)(2,1)} %param.17) | copy-start | bytes 7684
  15.0 1.0 copy-start.14
  16.0 0.9 copy-start.16
  19.9 11.1 %all-to-all-start.1 = ((bf16[4,64,1280]{2,1,0:T(8,128)(2,1)}), bf16[4,64,1280]{2,1,0:T(8,128)(2,1)S(1)}, u32[]{:S(2)}, u32[]{:S(2)}) async-start(bf16[4,64,1280]{2,1,0:T(8,128)(2,1)} %get-tuple-element.24), calls=%async_computation.1 | async-start | bytes 1310720 | tf_op jit(solution)/shard_map/all_to_all | solution.py:219
  32.4 8.1 %all-to-all-start.2 = ((bf16[4,64,256]{2,1,0:T(8,128)(2,1)}), bf16[4,64,256]{2,1,0:T(8,128)(2,1)S(1)}, u32[]{:S(2)}, u32[]{:S(2)}) async-start(bf16[4,64,256]{2,1,0:T(8,128)(2,1)} %shard_map.134), calls=%async_computation.2 | async-start | bytes 262144 | tf_op jit(solution)/shard_map/all_to_all | solution.py:219
  40.5 0.9 copy-start.4
  41.4 0.9 copy-start.6
  43.2 38.1 %all-to-all-start.3 = ((bf16[128,4,128]{2,1,0:T(4,128)(2,1)}), bf16[128,4,128]{2,1,0:T(4,128)(2,1)S(1)}, u32[]{:S(2)}, u32[]{:S(2)}) async-start(bf16[128,4,128]{2,1,0:T(4,128)(2,1)} %bitcast.12), calls=%async_computation.3 | async-start | bytes 262144 | tf_op jit(solution)/shard_map/all_to_all | solution.py:219
  68.1 1.0 copy-start.10
  69.2 1.0 copy-start.12
  70.2 11.0 %copy-start.11 = (bf16[256,1024]{1,0:T(8,128)(2,1)S(1)}, bf16[256,1024]{1,0:T(8,128)(2,1)}, u32[]{:S(2)}) copy-start(bf16[256,1024]{1,0:T(8,128)(2,1)} %q_ref.3) | copy-start | bytes 1572868
  72.2 1.0 copy-start.19
  73.2 0.8 copy-start.21
  74.0 0.8 copy-start.23
  74.8 0.8 copy-start.25
  75.6 0.8 copy-start.27
  81.2 1.0 copy-start.13
  82.3 1.0 copy-start.22
  83.3 1.0 copy-start.24
  84.4 1.0 copy-start.26
  85.4 1.0 copy-start.28
  86.5 26.3 %copy-start.2 = (bf16[128,512]{1,0:T(8,128)(2,1)S(1)}, bf16[128,512]{1,0:T(8,128)(2,1)}, u32[]{:S(2)}) copy-start(bf16[128,512]{1,0:T(8,128)(2,1)} %copy-done.1) | copy-start | bytes 393220
  90.0 1.0 copy-start.17
  113.6 8.1 %all-to-all-start.5 = ((bf16[4,64,256]{2,1,0:T(8,128)(2,1)}), bf16[4,64,256]{2,1,0:T(8,128)(2,1)S(1)}, u32[]{:S(2)}, u32[]{:S(2)}) async-start(bf16[4,64,256]{2,1,0:T(8,128)(2,1)} %shard_map.138), calls=%async_computation.5 | async-start | bytes 262144 | tf_op jit(solution)/shard_map/all_to_all | solution.py:219
  116.9 1.2 copy-start.18
  118.2 1.2 copy-start.20
  (3 other events, 1.9 us)

commit v2 on v1

v2 whole, which is shorter than its diff:
```python
import math

import jax
import jax.numpy as jnp
from jax import lax
from jax.experimental import pallas as pl
from jax.experimental.pallas import tpu as pltpu
from jax.sharding import PartitionSpec as P

VIT_HD = 80
HD = 128
EPS = 1e-6
NEG = -1e30
EMPTY = 2.0**100
WIDE = 59
LOG2E = math.log2(math.e)
SCALE2 = LOG2E / math.sqrt(HD)
F32 = jnp.float32
BF16 = jnp.bfloat16
VM = pl.BlockSpec(memory_space=pltpu.VMEM)
SM = pl.BlockSpec(memory_space=pltpu.SMEM)
ANY = pl.BlockSpec(memory_space=pl.ANY)
DMA = pltpu.SemaphoreType.DMA


def dot(a, b):
    return jnp.dot(a, b, preferred_element_type=F32)


def iota(shape, dim):
    return lax.broadcasted_iota(jnp.int32, shape, dim)


def call(kernel, out_shape, *args, flops=0, moved=0, limit=6, specs=None, out_specs=None, scratch=()):
    return pl.pallas_call(
        kernel,
        out_shape=out_shape,
        in_specs=specs or [VM] * len(args),
        out_specs=out_specs or jax.tree.map(lambda _: VM, out_shape),
        scratch_shapes=scratch,
        compiler_params=limit and pltpu.CompilerParams(vmem_limit_bytes=limit * 2**20),
        cost_estimate=pl.CostEstimate(flops=flops, bytes_accessed=moved, transcendentals=0),
    )(*args)


def shape(dims, dtype=BF16):
    return jax.ShapeDtypeStruct(dims, dtype)


def one_hot(mask):
    return mask.astype(F32).astype(BF16)


def fetch(pairs, sems):
    copies = [pltpu.make_async_copy(a, b, sems.at[i]) for i, (a, b) in enumerate(pairs)]
    for copy in copies:
        copy.start()
    return copies


def code_kernel(rows_ref, dest_ref, code_ref):
    pieces = rows_ref.shape[1]
    a = iota((pieces, pieces), 0)
    b = iota((pieces, pieces), 1)
    rows = jnp.broadcast_to(rows_ref[...].astype(F32), (pieces, pieces))
    dest = jnp.broadcast_to(dest_ref[...].astype(F32), (pieces, pieces))
    starts = jnp.sum(jnp.where(b < a, rows, 0.0), axis=1, keepdims=True)
    count = jnp.sum(jnp.where(b == a, rows, 0.0), axis=1, keepdims=True)
    target = jnp.sum(jnp.where(b == a, dest, 0.0), axis=1, keepdims=True)
    lane = iota((pieces, HD), 1)
    row = (lane & 63).astype(F32)
    inside = (row >= starts) & (row < starts + count)
    code = jnp.sum(jnp.where(inside, target * 4.0 + row - starts, 0.0), axis=0, keepdims=True)
    code_ref[...] = jnp.broadcast_to(code, (8, HD)) + 2.0 * (iota((8, HD), 1) >> 6).astype(F32)


def vit_kernel(
    pos_ref, gain_hbm, win_hbm, wt_hbm, x_hbm, proj_hbm, part_ref, own_ref,
    gain_ref, win_ref, wt_ref, x_ref, proj_ref, w_ref, sems,
):
    pairs = [(gain_hbm, gain_ref), (x_hbm, x_ref), (wt_hbm, wt_ref)]
    pairs += [(win_hbm, win_ref), (proj_hbm, proj_ref)]
    copies = fetch(pairs, sems)
    width, points = x_ref.shape
    copies[0].wait()
    copies[1].wait()
    x = x_ref[...]
    local = proj_ref.shape[0]
    xf = x.astype(F32)
    scale = lax.rsqrt(jnp.sum(xf * xf, axis=0, keepdims=True) * (1.0 / width) + EPS)
    copies[2].wait()
    for i in range(width // HD):
        cols = slice(i * HD, (i + 1) * HD)
        w_ref[:, cols] = (wt_ref[:, cols].astype(F32) * gain_ref[i : i + 1].astype(F32)).astype(BF16)
    qkv = (dot(w_ref[...], x) * scale).astype(BF16)
    copies[3].wait()
    wins = jnp.broadcast_to(win_ref[...].astype(F32), (8, points))
    bias = jnp.where(wins.T[:, :1] == wins[:1], 0.0, NEG)
    mixed = []
    for h in range(local // VIT_HD):
        q = qkv[h * VIT_HD : (h + 1) * VIT_HD]
        k = qkv[local + h * VIT_HD : local + (h + 1) * VIT_HD]
        v = qkv[2 * local + h * VIT_HD : 2 * local + (h + 1) * VIT_HD]
        s = dot(k.T, q) * (LOG2E / math.sqrt(VIT_HD)) + bias
        e = jnp.exp2(s - jnp.max(s, axis=0, keepdims=True))
        weights = (e * (1.0 / jnp.sum(e, axis=0, keepdims=True))).astype(BF16)
        mixed.append(dot(v, weights).astype(BF16))
    mixed = jnp.concatenate(mixed, axis=0)
    n = iota((points, points), 1)
    perm = one_hot(iota((points, points), 0) == 4 * (n & 63) + (n >> 6))
    mixed = dot(mixed, perm).astype(BF16)
    copies[4].wait()
    part = dot(mixed.T, proj_ref[...]).astype(BF16)
    for m in range(4):
        part_ref[m] = part[m * 64 : (m + 1) * 64]
    sel = one_hot(iota((points, 64), 0) == 4 * iota((points, 64), 1) + pos_ref[0])
    own_ref[...] = dot(x, sel).astype(BF16).T


def merge_kernel(in_ref, own_ref, gain_ref, w_ref, out_ref):
    resid = own_ref[...].astype(F32)
    for m in range(4):
        resid = resid + in_ref[m].astype(F32)
    scale = lax.rsqrt(jnp.mean(resid * resid, axis=1, keepdims=True) + EPS)
    merged = (resid * scale * gain_ref[...].astype(F32)).astype(BF16)
    kv = dot(merged, w_ref[...]).astype(BF16)
    for h in range(4):
        out_ref[h] = kv[:, h * 256 : (h + 1) * 256]


def pack_kernel(in_ref, code_hbm, out_ref, code_ref, sems):
    copies = fetch([(code_hbm, code_ref)], sems)
    kv = in_ref[0].astype(F32)
    for m in range(1, 4):
        kv = kv + in_ref[m].astype(F32)
    kv = kv.astype(BF16)
    stack = jnp.concatenate([kv[:, :HD], kv[:, HD:]], axis=0)
    copies[0].wait()
    dims = out_ref.shape
    row = iota(dims, 0)
    picks = one_hot(row.astype(F32) == code_ref[:1])
    filled = dot(picks, jnp.ones((HD, HD), BF16))
    empty = jnp.where(((row & 2) == 0) & (filled < 0.5), EMPTY, 0.0)
    out_ref[...] = (dot(picks, stack) + empty).astype(BF16)


def halves(ref):
    half = ref.shape[1] // 2
    return [ref.at[:, :half], ref.at[:, half:]]


def fetch_wide(q_hbm, c_hbm, q_ref, c_ref, sems):
    pairs = list(zip(halves(q_hbm) + halves(c_hbm), halves(q_ref) + halves(c_ref)))
    q0, q1, c0, c1 = pairs
    return fetch([q0, c0, q1, c1], sems)


def text_kernel(kv_hbm, q_hbm, c_hbm, stats_ref, kv_ref, q_ref, c_ref, sems):
    head = fetch([(kv_hbm, kv_ref)], sems.at[pl.ds(0, 1)])[0]
    copies = fetch_wide(q_hbm, c_hbm, q_ref, c_ref, sems.at[pl.ds(1, 4)])
    group = q_ref.shape[1] // HD
    rows = q_ref.shape[0]
    head.wait()
    k, v = text_pair(kv_ref)
    causal = iota((rows, rows), 0) <= iota((rows, rows), 1)
    for g in range(group):
        if g % (group // 2) == 0:
            for copy in copies[:2] if g == 0 else copies[2:]:
                copy.wait()
        s = jnp.where(causal, dot(k, q_ref[:, g * HD : (g + 1) * HD].T) * SCALE2, NEG)
        m = jnp.max(s, axis=0, keepdims=True)
        e = jnp.exp2(s - m)
        dp = dot(v, c_ref[:, g * HD : (g + 1) * HD].T)
        stats_ref[g : g + 1] = m
        stats_ref[group + g : group + g + 1] = jnp.sum(e, axis=0, keepdims=True)
        stats_ref[2 * group + g : 2 * group + g + 1] = jnp.sum(e * dp, axis=0, keepdims=True)


def text_pair(kv_ref):
    a = iota((HD, HD), 0)
    order = one_hot(iota((HD, HD), 1) == 2 * (a & 63) + (a >> 6))
    return split(order, kv_ref)


def split(order, ref):
    keys = []
    values = []
    for b in range(ref.shape[0] // HD):
        part = dot(order, ref[b * HD : (b + 1) * HD]).astype(BF16)
        keys.append(part[:64])
        values.append(part[64:])
    return jnp.concatenate(keys, axis=0), jnp.concatenate(values, axis=0)


def slot_place(j):
    return 4 * ((j & 63) >> 1) + 2 * (j >> 6) + (j & 1)


def slot_pair(in_ref):
    order = one_hot(iota((HD, HD), 1) == slot_place(iota((HD, HD), 0)))
    keys, values = split(order, in_ref)
    live = jnp.broadcast_to(keys[:, :1].astype(F32) < 0.5 * EMPTY, keys.shape)
    bias = jnp.where(live, 0.0, NEG)
    keys = jnp.where(live, keys.astype(F32), 0.0).astype(BF16)
    return keys, values, jnp.concatenate([bias, bias], axis=1)


def slots_kernel(
    in_hbm, text_hbm, q_hbm, c_hbm, out_ref, stats_ref, in_ref, text_ref, q_ref, c_ref, sems
):
    head, stats = fetch([(in_hbm, in_ref), (text_hbm, text_ref)], sems.at[pl.ds(0, 2)])
    copies = fetch_wide(q_hbm, c_hbm, q_ref, c_ref, sems.at[pl.ds(2, 4)])
    group = q_ref.shape[1] // HD
    head.wait()
    k, v, bias = slot_pair(in_ref)
    slots = k.shape[0]
    stats.wait()
    dk = jnp.zeros((slots, HD), F32)
    dv = jnp.zeros((slots, HD), F32)
    for g in range(group):
        if g % (group // 2) == 0:
            for copy in copies[:2] if g == 0 else copies[2:]:
                copy.wait()
        q = q_ref[:, g * HD : (g + 1) * HD]
        c = c_ref[:, g * HD : (g + 1) * HD]
        s = dot(k, q.T) * SCALE2 + bias
        dp = dot(v, c.T)
        mt = text_ref[g : g + 1]
        m = jnp.maximum(mt, jnp.max(s, axis=0, keepdims=True))
        e = jnp.exp2(s - m)
        alpha = jnp.exp2(mt - m)
        total = text_ref[group + g : group + g + 1] * alpha + jnp.sum(e, axis=0, keepdims=True)
        inv = 1.0 / total
        delta = text_ref[2 * group + g : 2 * group + g + 1] * alpha
        delta = (delta + jnp.sum(e * dp, axis=0, keepdims=True)) * inv
        stats_ref[g : g + 1] = m
        stats_ref[group + g : group + g + 1] = inv
        p = e * inv
        ds = (p * (dp - delta)).astype(BF16)
        dk = dk + dot(ds, q)
        dv = dv + dot(p.astype(BF16), c)
    dk = (dk * (1.0 / math.sqrt(HD))).astype(BF16)
    dv = dv.astype(BF16)
    order = one_hot(iota((HD, HD), 0) == slot_place(iota((HD, HD), 1)))
    for b in range(slots // 64):
        pair = jnp.concatenate([dk[b * 64 : (b + 1) * 64], dv[b * 64 : (b + 1) * 64]], axis=0)
        out_ref[b * HD : (b + 1) * HD] = dot(order, pair).astype(BF16)


def output_kernel(
    in_hbm, kv_hbm, stats_hbm, q_hbm, out_ref, in_ref, kv_ref, stats_ref, q_ref, sems
):
    pairs = [(in_hbm, in_ref), (kv_hbm, kv_ref), (stats_hbm, stats_ref), (q_hbm, q_ref)]
    for copy in fetch(pairs, sems):
        copy.wait()
    group = q_ref.shape[1] // HD
    rows = q_ref.shape[0]
    kt, vt = text_pair(kv_ref)
    ks, vs, bias = slot_pair(in_ref)
    vt = vt.T
    vs = vs.T
    causal = iota((rows, rows), 0) <= iota((rows, rows), 1)
    for g in range(group):
        qt = q_ref[:, g * HD : (g + 1) * HD].T
        m = stats_ref[g : g + 1]
        inv = stats_ref[group + g : group + g + 1]
        s = jnp.where(causal, dot(kt, qt) * SCALE2, NEG)
        o = dot(vt, (jnp.exp2(s - m) * inv).astype(BF16))
        s = dot(ks, qt) * SCALE2 + bias
        o = o + dot(vs, (jnp.exp2(s - m) * inv).astype(BF16))
        out_ref[:, g * HD : (g + 1) * HD] = o.T.astype(BF16)


def rows_kernel(in_ref, code_ref, out_ref):
    code = jnp.broadcast_to(code_ref[:1], (HD, HD)).T
    count = in_ref.shape[0]
    picks = one_hot(iota((HD, count), 1).astype(F32) == code[:, :1])
    g = dot(picks, in_ref[...]).astype(BF16)
    half = HD // 2
    for m in range(4):
        out_ref[m, :, :HD] = g[:half]
        out_ref[m, :, HD:] = g[half:]


def fold_kernel(in_ref, w_ref, out_ref):
    grads = jnp.concatenate([in_ref[h] for h in range(4)], axis=1)
    out_ref[...] = dot(w_ref[...], grads.T).T.astype(BF16)


def exchange(x, axes):
    return lax.all_to_all(x, axes, split_axis=0, concat_axis=0, tiled=True)


def on_device(
    patches, window_index, vit_gain, vit_qkv, vit_proj, merge_gain, piece_rows, piece_dest,
    visual_kv, text_query, text_kv, out_cotangent,
):
    shards = lax.axis_size("sec") * lax.axis_size("dp")
    position = lax.axis_index("mp").astype(jnp.int32).reshape(1)
    points, width_part = patches.shape
    width = vit_qkv.shape[0]
    local = vit_qkv.shape[2]
    rows = text_query.shape[0]
    slots = 2 * shards
    merged_rows = points // 4

    x = lax.all_gather(patches.T, "mp", axis=0, tiled=True)
    wt = jnp.transpose(vit_qkv, (1, 2, 0)).reshape(3 * local, width)
    part, own = call(
        vit_kernel, (shape((4, merged_rows, width)), shape((merged_rows, width))),
        position, vit_gain.reshape(-1, HD), window_index.reshape(1, points), wt, x, vit_proj,
        specs=[SM] + [ANY] * 5, limit=WIDE, flops=10**9, moved=4 * 10**6,
        scratch=[
            pltpu.VMEM((width // HD, HD), BF16), pltpu.VMEM((1, points), jnp.int32),
            pltpu.VMEM((3 * local, width), BF16), pltpu.VMEM((width, points), BF16),
            pltpu.VMEM((local, width), BF16), pltpu.VMEM((3 * local, width), BF16), DMA((5,)),
        ],
    )
    code = call(
        code_kernel, shape((8, HD), F32), piece_rows.reshape(1, -1), piece_dest.reshape(1, -1),
        flops=10**6, moved=10**4,
    )
    summed = exchange(part, "mp")
    w_kv = jnp.transpose(visual_kv.reshape(width, 2, 4, HD), (0, 2, 1, 3)).reshape(width, 8 * HD)
    kv_part = call(
        merge_kernel, shape((4, merged_rows, 2 * HD)),
        summed, own, merge_gain.reshape(1, width), w_kv, flops=2 * 10**8, moved=4 * 10**6,
    )
    kv_terms = exchange(kv_part, "mp")
    group = text_query.shape[1] // HD
    text_rows = text_kv.reshape(2 * rows, HD)
    wide = pltpu.VMEM((rows, group * HD), BF16)
    thin = pltpu.VMEM((2 * rows, HD), BF16)
    stats = call(
        text_kernel, shape((3 * group, rows), F32), text_rows, text_query, out_cotangent,
        specs=[ANY] * 3, scratch=[thin, wide, wide, DMA((5,))], limit=WIDE,
        flops=10**9, moved=2 * 10**6,
    )
    kv_terms, stats = lax.optimization_barrier((kv_terms, stats))
    outgoing = call(
        pack_kernel, shape((2 * slots, HD)), kv_terms, code, specs=[VM, ANY],
        scratch=[pltpu.VMEM((8, HD), F32), DMA((1,))], flops=2 * 10**7, moved=10**6,
    )
    route = ("sec", "dp")
    incoming = exchange(outgoing.reshape(shards, 4, HD), route).reshape(2 * slots, HD)
    slot_rows = pltpu.VMEM(incoming.shape, BF16)
    grads, stats = call(
        slots_kernel, (shape((2 * slots, HD)), shape((2 * group, rows), F32)),
        incoming, stats, text_query, out_cotangent, specs=[ANY] * 4, limit=WIDE,
        scratch=[slot_rows, pltpu.VMEM(stats.shape, F32), wide, wide, DMA((6,))],
        flops=10**9, moved=2 * 10**6,
    )
    returned = exchange(grads.reshape(shards, 4, HD), route).reshape(2 * slots, HD)
    attended = call(
        output_kernel, shape((rows, group * HD)), incoming, text_rows, stats, text_query,
        specs=[ANY] * 4, scratch=[slot_rows, thin, pltpu.VMEM(stats.shape, F32), wide, DMA((4,))],
        limit=WIDE, flops=10**9, moved=2 * 10**6,
    )
    returned, attended = lax.optimization_barrier((returned, attended))
    row_grads = call(
        rows_kernel, shape((4, merged_rows, 2 * HD)), returned, code, flops=2 * 10**7, moved=5 * 10**5,
    )
    heads = exchange(row_grads, "mp")
    visual_grad = call(
        fold_kernel, shape((merged_rows, width)), heads, w_kv, flops=2 * 10**8, moved=3 * 10**6,
    )
    return (attended, visual_grad)


def solution(mesh):
    both = ("sec", "dp")
    in_specs = (
        P(both, "mp"), P(both), P(), P(None, None, "mp"), P("mp", None), P(), P(both), P(both),
        P("mp", None, None), P(both, "mp"), P(both, None, "mp"), P(both, "mp"),
    )
    return jax.shard_map(
        on_device, mesh=mesh, in_specs=in_specs, out_specs=(P(both, "mp"), P(both, "mp")),
        check_vma=False,
    )
```

time: 125 us -> 110 us (0.88)
  blocking collectives: 21.7 us -> 56.5 us
  local copies, waits for them, and re-layouts: 31.3 us -> 4.31 us
  starting transfers between devices: 39.9 us -> 13.1 us
  Pallas kernels: 15 us -> 20.9 us
    all_to_all x5 -> x3, starting transfers between devices: 39.9 us -> 13.1 us  [exchange(): return lax.all_to_all(x, axes, split_axis=0, concat_axis=0, tiled=True)]
    unnamed x60 -> x8, local copies, waits for them, and re-layouts: 23.3 us -> 0.02 us
    all_to_all x1 -> x2, blocking collectives: 21.7 us -> 42.8 us  [exchange(): return lax.all_to_all(x, axes, split_axis=0, concat_axis=0, tiled=True)]
    all_gather x0 -> x1, blocking collectives: none -> 13.7 us  [on_device(): x = lax.all_gather(patches.T, 'mp', axis=0, tiled=True)]
    pallas_call x9, Pallas kernels: 15 us -> 20.9 us  [call(): pl.pallas_call(kernel, out_shape=out_shape, in_specs=specs or [VM] * len(...]
    broadcast_in_dim x1 -> x0, local copies, waits for them, and re-layouts: 1.89 us -> none  [on_device(): jnp.broadcast_to(patches.T[None], (4, width_part, points))]
    all_to_all x5 -> x3, waiting for transfers between devices: 14.5 us -> 13.6 us  [exchange(): return lax.all_to_all(x, axes, split_axis=0, concat_axis=0, tiled=True)]
  transfers between devices with their start and end apart: 5 -> 3, of which waited for: 5 -> 3; matrix products, arithmetic and copies ran while one was open for 5% -> 4% of each run, Pallas kernels for 3% -> 7%
where the time goes in v2:
time: 110 us; the launch traced here: 109 us
  blocking collectives  56.5 us (51%)
  Pallas kernels  20.9 us (19%)
  waiting for transfers between devices  13.6 us (12%)
  starting transfers between devices  13.1 us (12%)
  local copies, waits for them, and re-layouts  4.31 us (4%)
    all_to_all x2, blocking collectives, exchange(): return lax.all_to_all(x, axes, split_axis=0, concat_axis=0, tiled=True)  42.8 us
    pallas_call x9, Pallas kernels, call(): pl.pallas_call(kernel, out_shape=out_shape, in_specs=specs or [VM] * len(...  20.9 us
    all_gather x1, blocking collectives, on_device(): x = lax.all_gather(patches.T, 'mp', axis=0, tiled=True)  13.7 us
    all_to_all x3, waiting for transfers between devices, exchange(): return lax.all_to_all(x, axes, split_axis=0, concat_axis=0, tiled=True)  13.6 us
    all_to_all x3, starting transfers between devices, exchange(): return lax.all_to_all(x, axes, split_axis=0, concat_axis=0, tiled=True)  13.1 us
    reshape x1, local copies, waits for them, and re-layouts, on_device(): jnp.transpose(visual_kv.reshape(width, 2, 4, HD), (0, 2, 1, 3))  4.28 us
  transfers between devices with their start and end apart: 3, of which 3 were waited for; matrix products, arithmetic and copies ran while one was open for 4% of the time, Pallas kernels for 7%

profile of v2, /device:TPU:1, one launch (start us, length us, event | category | flops | bytes accessed | tf_op | source)
XLA Modules:
  0.0 109.2 jit_solution(5275114687356779702)
XLA Ops:
  0.6 13.7 %all_gather.3.x_hbm = bf16[1280,256]{1,0:T(8,128)(2,1)} all-gather(bf16[320,256]{1,0:T(8,128)(2,1)} %bitcast.22), channel_id=1, replica_groups=mesh['sec'=2,'dp'=64,'mp'=4] {'mp'}, dimensions={0}, use_global_device_ids=true | all-gather | bytes 819200 | tf_op jit(solution)/shard_map/all_gather | solution.py:307
  14.3 0.0 copy-start.3
  14.3 4.7 %shard_map.131 = (bf16[4,64,1280]{2,1,0:T(8,128)(2,1)}, bf16[64,1280]{1,0:T(8,128)(2,1)}) custom-call(s32[1]{0:T(128)} %bitcast.pos_ref, bf16[10,128]{1,0:T(8,128)(2,1)} %bitcast.29, s32[1,256]{1,0:T(1,128)} %bitcast.30, bf16[480,1280]{1,0:T(8,128)(2,1)} %bitcast.26, bf16[1280,256]{1,0:T(8,128)(2,1)} %all_gather.3.x_hbm, bf16[160,1280]{1,0:T(8,128)(2,1)} %proj_hbm.1), custom_call_target="tpu_custom_call" | custom-call | flops 1000000000 | bytes 4000000 | tf_op jit(solution)/shard_map/pallas_call | solution.py:35
  19.0 3.5 %all-to-all-start = ((bf16[4,64,1280]{2,1,0:T(8,128)(2,1)}), bf16[4,64,1280]{2,1,0:T(8,128)(2,1)S(1)}, u32[]{:S(2)}, u32[]{:S(2)}) async-start(bf16[4,64,1280]{2,1,0:T(8,128)(2,1)} %get-tuple-element.10), calls=%async_computation | async-start | bytes 1310720 | tf_op jit(solution)/shard_map/all_to_all | solution.py:291
  22.5 0.0 copy-done.3
  22.6 0.0 copy-start
  22.6 4.3 %reshape.52.w_ref = bf16[1280,1024]{1,0:T(8,128)(2,1)S(1)} reshape(bf16[1280,4,2,128]{3,2,1,0:T(2,128)(2,1)} %bitcast.21) | data formatting | bytes 5242880 | tf_op jit(solution)/shard_map/reshape | solution.py:324
  26.9 0.0 copy-start.1
  26.9 0.0 copy-start.2
  26.9 3.3 %all-to-all-done.in_ref = bf16[4,64,1280]{2,1,0:T(8,128)(2,1)S(1)} async-done(((bf16[4,64,1280]{2,1,0:T(8,128)(2,1)}), bf16[4,64,1280]{2,1,0:T(8,128)(2,1)S(1)}, u32[]{:S(2)}, u32[]{:S(2)}) %all-to-all-start) | async-done | bytes 655392 | tf_op jit(solution)/shard_map/all_to_all | solution.py:291
  30.1 0.0 copy-done
  30.1 1.4 %shard_map.132 = bf16[4,64,256]{2,1,0:T(8,128)(2,1)} custom-call(bf16[4,64,1280]{2,1,0:T(8,128)(2,1)S(1)} %all-to-all-done.in_ref, bf16[64,1280]{1,0:T(8,128)(2,1)S(1)} %copy-done, bf16[1,1280]{1,0:T(2,128)(2,1)S(1)} %reshape.50.gain_ref, bf16[1280,1024]{1,0:T(8,128)(2,1)S(1)} %reshape.52.w_ref), custom_call_target="tpu_custom_call" | custom-call | flops 200000000 | bytes 4000000 | tf_op jit(solution)/shard_map/pallas_call | solution.py:35
  31.5 3.3 %all-to-all-start.1 = ((bf16[4,64,256]{2,1,0:T(8,128)(2,1)}), bf16[4,64,256]{2,1,0:T(8,128)(2,1)S(1)}, u32[]{:S(2)}, u32[]{:S(2)}) async-start(bf16[4,64,256]{2,1,0:T(8,128)(2,1)} %shard_map.132), calls=%async_computation.1 | async-start | bytes 262144 | tf_op jit(solution)/shard_map/all_to_all | solution.py:291
  34.9 0.0 copy-done.1
  34.9 0.0 copy-done.2
  34.9 0.1 shard_map.134.code_hbm.code_ref
  35.0 2.8 %shard_map.133.text_hbm = f32[24,256]{1,0:T(8,128)} custom-call(bf16[512,128]{1,0:T(8,128)(2,1)} %bitcast.27, bf16[256,1024]{1,0:T(8,128)(2,1)} %q_hbm.5, bf16[256,1024]{1,0:T(8,128)(2,1)} %c_hbm.3), custom_call_target="tpu_custom_call" | custom-call | flops 1000000000 | bytes 2000000 | tf_op jit(solution)/shard_map/pallas_call | solution.py:35
  37.8 1.8 %all-to-all-done.1.in_ref = bf16[4,64,256]{2,1,0:T(8,128)(2,1)S(1)} async-done(((bf16[4,64,256]{2,1,0:T(8,128)(2,1)}), bf16[4,64,256]{2,1,0:T(8,128)(2,1)S(1)}, u32[]{:S(2)}, u32[]{:S(2)}) %all-to-all-start.1) | async-done | bytes 131104 | tf_op jit(solution)/shard_map/all_to_all | solution.py:291
  39.7 0.2 shard_map.135
  39.9 35.6 %all_to_all.25 = bf16[128,4,128]{2,1,0:T(4,128)(2,1)} all-to-all(bf16[128,4,128]{2,1,0:T(4,128)(2,1)S(1)} %bitcast.18), channel_id=1, replica_groups=mesh['sec'=2,'dp'=64,'mp'=4] {'sec','dp'}, dimensions={0} | all-to-all | bytes 262144 | tf_op jit(solution)/shard_map/all_to_all | solution.py:291
  75.5 5.1 %shard_map.136 = (bf16[512,128]{1,0:T(8,128)(2,1)}, f32[16,256]{1,0:T(8,128)}) custom-call(bf16[512,128]{1,0:T(8,128)(2,1)} %bitcast.23, f32[24,256]{1,0:T(8,128)} %shard_map.133.text_hbm, bf16[256,1024]{1,0:T(8,128)(2,1)} %q_hbm.5, bf16[256,1024]{1,0:T(8,128)(2,1)} %c_hbm.3), custom_call_target="tpu_custom_call" | custom-call | flops 1000000000 | bytes 2000000 | tf_op jit(solution)/shard_map/pallas_call | solution.py:35
  80.7 6.3 %all-to-all-start.3 = ((bf16[128,4,128]{2,1,0:T(4,128)(2,1)}), bf16[128,4,128]{2,1,0:T(4,128)(2,1)S(1)}, u32[]{:S(2)}, u32[]{:S(2)}) async-start(bf16[128,4,128]{2,1,0:T(4,128)(2,1)} %bitcast.25), calls=%async_computation.3 | async-start | bytes 262144 | tf_op jit(solution)/shard_map/all_to_all | solution.py:291
  86.9 4.6 %shard_map.137 = bf16[256,1024]{1,0:T(8,128)(2,1)} custom-call(bf16[512,128]{1,0:T(8,128)(2,1)} %bitcast.24, bf16[512,128]{1,0:T(8,128)(2,1)} %bitcast.28, f32[16,256]{1,0:T(8,128)} %get-tuple-element.15.stats_hbm, bf16[256,1024]{1,0:T(8,128)(2,1)} %q_hbm.5), custom_call_target="tpu_custom_call" | custom-call | flops 1000000000 | bytes 2000000 | tf_op jit(solution)/shard_map/pallas_call | solution.py:35
  91.6 8.5 %all-to-all-done.3 = bf16[128,4,128]{2,1,0:T(4,128)(2,1)S(1)} async-done(((bf16[128,4,128]{2,1,0:T(4,128)(2,1)}), bf16[128,4,128]{2,1,0:T(4,128)(2,1)S(1)}, u32[]{:S(2)}, u32[]{:S(2)}) %all-to-all-start.3) | async-done | bytes 131104 | tf_op jit(solution)/shard_map/all_to_all | solution.py:291
  100.1 0.3 shard_map.138
  100.4 7.2 %all_to_all.26.in_ref = bf16[4,64,256]{2,1,0:T(8,128)(2,1)S(1)} all-to-all(bf16[4,64,256]{2,1,0:T(8,128)(2,1)S(1)} %shard_map.138), channel_id=1, replica_groups=mesh['sec'=2,'dp'=64,'mp'=4] {'mp'}, dimensions={0} | all-to-all | bytes 262144 | tf_op jit(solution)/shard_map/all_to_all | solution.py:291
  107.6 1.5 %shard_map.139 = bf16[64,1280]{1,0:T(8,128)(2,1)} custom-call(bf16[4,64,256]{2,1,0:T(8,128)(2,1)S(1)} %all_to_all.26.in_ref, bf16[1280,1024]{1,0:T(8,128)(2,1)S(1)} %reshape.52.w_ref), custom_call_target="tpu_custom_call" | custom-call | flops 200000000 | bytes 3000000 | tf_op jit(solution)/shard_map/pallas_call | solution.py:35
  (1 shorter events, 0.0 us)
Async XLA Ops:
  14.3 8.2 %copy-start.3 = (bf16[1280]{0:T(1024)(128)(2,1)S(1)}, bf16[1280]{0:T(1024)(128)(2,1)}, u32[]{:S(2)}) copy-start(bf16[1280]{0:T(1024)(128)(2,1)} %param.17) | copy-start | bytes 7684
  19.0 11.1 %all-to-all-start = ((bf16[4,64,1280]{2,1,0:T(8,128)(2,1)}), bf16[4,64,1280]{2,1,0:T(8,128)(2,1)S(1)}, u32[]{:S(2)}, u32[]{:S(2)}) async-start(bf16[4,64,1280]{2,1,0:T(8,128)(2,1)} %get-tuple-element.10), calls=%async_computation | async-start | bytes 1310720 | tf_op jit(solution)/shard_map/all_to_all | solution.py:291
  22.6 7.6 %copy-start = (bf16[64,1280]{1,0:T(8,128)(2,1)S(1)}, bf16[64,1280]{1,0:T(8,128)(2,1)}, u32[]{:S(2)}) copy-start(bf16[64,1280]{1,0:T(8,128)(2,1)} %get-tuple-element.11.own_ref) | copy-start | bytes 491524
  26.9 8.0 %copy-start.1 = (s32[64]{0:T(128)S(1)}, s32[64]{0:T(128)}, u32[]{:S(2)}) copy-start(s32[64]{0:T(128)} %param.18) | copy-start | bytes 772
  26.9 8.0 %copy-start.2 = (s32[64]{0:T(128)S(1)}, s32[64]{0:T(128)}, u32[]{:S(2)}) copy-start(s32[64]{0:T(128)} %param.19) | copy-start | bytes 772
  31.5 8.1 %all-to-all-start.1 = ((bf16[4,64,256]{2,1,0:T(8,128)(2,1)}), bf16[4,64,256]{2,1,0:T(8,128)(2,1)S(1)}, u32[]{:S(2)}, u32[]{:S(2)}) async-start(bf16[4,64,256]{2,1,0:T(8,128)(2,1)} %shard_map.132), calls=%async_computation.1 | async-start | bytes 262144 | tf_op jit(solution)/shard_map/all_to_all | solution.py:291
  80.7 19.4 %all-to-all-start.3 = ((bf16[128,4,128]{2,1,0:T(4,128)(2,1)}), bf16[128,4,128]{2,1,0:T(4,128)(2,1)S(1)}, u32[]{:S(2)}, u32[]{:S(2)}) async-start(bf16[128,4,128]{2,1,0:T(4,128)(2,1)} %bitcast.25), calls=%async_computation.3 | async-start | bytes 262144 | tf_op jit(solution)/shard_map/all_to_all | solution.py:291

commit v3 on v2

--- a/solution.py
+++ b/solution.py
@@ -13,6 +13,8 @@
 NEG = -1e30
 EMPTY = 2.0**100
 WIDE = 59
+DP = 64
+SLOTL = 53.5
 LOG2E = math.log2(math.e)
 SCALE2 = LOG2E / math.sqrt(HD)
 F32 = jnp.float32
@@ -38,7 +40,7 @@
         in_specs=specs or [VM] * len(args),
         out_specs=out_specs or jax.tree.map(lambda _: VM, out_shape),
         scratch_shapes=scratch,
-        compiler_params=limit and pltpu.CompilerParams(vmem_limit_bytes=limit * 2**20),
+        compiler_params=limit and pltpu.CompilerParams(vmem_limit_bytes=int(limit * 2**20)),
         cost_estimate=pl.CostEstimate(flops=flops, bytes_accessed=moved, transcendentals=0),
     )(*args)
 
@@ -63,7 +65,9 @@
     a = iota((pieces, pieces), 0)
     b = iota((pieces, pieces), 1)
     rows = jnp.broadcast_to(rows_ref[...].astype(F32), (pieces, pieces))
-    dest = jnp.broadcast_to(dest_ref[...].astype(F32), (pieces, pieces))
+    place = dest_ref[...]
+    place = (place & (DP - 1)) * 2 + (place >> (DP.bit_length() - 1))
+    dest = jnp.broadcast_to(place.astype(F32), (pieces, pieces))
     starts = jnp.sum(jnp.where(b < a, rows, 0.0), axis=1, keepdims=True)
     count = jnp.sum(jnp.where(b == a, rows, 0.0), axis=1, keepdims=True)
     target = jnp.sum(jnp.where(b == a, dest, 0.0), axis=1, keepdims=True)
@@ -144,6 +148,10 @@
     out_ref[...] = (dot(picks, stack) + empty).astype(BF16)
 
 
+def head_of(tall, ref):
+    return tall.at[pl.ds(0, ref.shape[0])]
+
+
 def halves(ref):
     half = ref.shape[1] // 2
     return [ref.at[:, :half], ref.at[:, half:]]
@@ -155,7 +163,7 @@
     return fetch([q0, c0, q1, c1], sems)
 
 
-def text_kernel(kv_hbm, q_hbm, c_hbm, stats_ref, kv_ref, q_ref, c_ref, sems):
+def text_kernel(kv_hbm, q_hbm, c_hbm, stats_hbm, kv_ref, q_ref, c_ref, stats_ref, sems):
     head = fetch([(kv_hbm, kv_ref)], sems.at[pl.ds(0, 1)])[0]
     copies = fetch_wide(q_hbm, c_hbm, q_ref, c_ref, sems.at[pl.ds(1, 4)])
     group = q_ref.shape[1] // HD
@@ -174,6 +182,7 @@
         stats_ref[g : g + 1] = m
         stats_ref[group + g : group + g + 1] = jnp.sum(e, axis=0, keepdims=True)
         stats_ref[2 * group + g : 2 * group + g + 1] = jnp.sum(e * dp, axis=0, keepdims=True)
+    fetch([(stats_ref, head_of(stats_hbm, stats_ref))], sems.at[pl.ds(5, 1)])[0].wait()
 
 
 def text_pair(kv_ref):
@@ -206,12 +215,14 @@
 
 
 def slots_kernel(
-    in_hbm, text_hbm, q_hbm, c_hbm, out_ref, stats_ref, in_ref, text_ref, q_ref, c_ref, sems
+    in_ref, text_hbm, q_hbm, c_hbm, out_ref, stats_hbm, in_hbm,
+    text_ref, q_ref, c_ref, stats_ref, sems,
 ):
-    head, stats = fetch([(in_hbm, in_ref), (text_hbm, text_ref)], sems.at[pl.ds(0, 2)])
-    copies = fetch_wide(q_hbm, c_hbm, q_ref, c_ref, sems.at[pl.ds(2, 4)])
+    copies = fetch_wide(q_hbm, c_hbm, q_ref, c_ref, sems.at[pl.ds(1, 4)])
+    pairs = [(head_of(text_hbm, text_ref), text_ref)]
+    stats = fetch(pairs, sems.at[pl.ds(0, 1)])[0]
+    kept = fetch([(in_ref, head_of(in_hbm, in_ref))], sems.at[pl.ds(6, 1)])[0]
     group = q_ref.shape[1] // HD
-    head.wait()
     k, v, bias = slot_pair(in_ref)
     slots = k.shape[0]
     stats.wait()
@@ -239,18 +250,22 @@
         ds = (p * (dp - delta)).astype(BF16)
         dk = dk + dot(ds, q)
         dv = dv + dot(p.astype(BF16), c)
+    sent = fetch([(stats_ref, head_of(stats_hbm, stats_ref))], sems.at[pl.ds(5, 1)])[0]
     dk = (dk * (1.0 / math.sqrt(HD))).astype(BF16)
     dv = dv.astype(BF16)
     order = one_hot(iota((HD, HD), 0) == slot_place(iota((HD, HD), 1)))
     for b in range(slots // 64):
         pair = jnp.concatenate([dk[b * 64 : (b + 1) * 64], dv[b * 64 : (b + 1) * 64]], axis=0)
         out_ref[b * HD : (b + 1) * HD] = dot(order, pair).astype(BF16)
+    sent.wait()
+    kept.wait()
 
 
 def output_kernel(
     in_hbm, kv_hbm, stats_hbm, q_hbm, out_ref, in_ref, kv_ref, stats_ref, q_ref, sems
 ):
-    pairs = [(in_hbm, in_ref), (kv_hbm, kv_ref), (stats_hbm, stats_ref), (q_hbm, q_ref)]
+    pairs = [(head_of(in_hbm, in_ref), in_ref), (kv_hbm, kv_ref), (q_hbm, q_ref)]
+    pairs += [(head_of(stats_hbm, stats_ref), stats_ref)]
     for copy in fetch(pairs, sems):
         copy.wait()
     group = q_ref.shape[1] // HD
@@ -331,9 +346,12 @@
     text_rows = text_kv.reshape(2 * rows, HD)
     wide = pltpu.VMEM((rows, group * HD), BF16)
     thin = pltpu.VMEM((2 * rows, HD), BF16)
+    tall = shape((4 * rows, rows), F32)
+    tall_slots = shape((16 * slots, HD))
     stats = call(
-        text_kernel, shape((3 * group, rows), F32), text_rows, text_query, out_cotangent,
-        specs=[ANY] * 3, scratch=[thin, wide, wide, DMA((5,))], limit=WIDE,
+        text_kernel, tall, text_rows, text_query, out_cotangent,
+        specs=[ANY] * 3, out_specs=ANY,
+        scratch=[thin, wide, wide, pltpu.VMEM((3 * group, rows), F32), DMA((6,))], limit=WIDE,
         flops=10**9, moved=2 * 10**6,
     )
     kv_terms, stats = lax.optimization_barrier((kv_terms, stats))
@@ -341,19 +359,23 @@
         pack_kernel, shape((2 * slots, HD)), kv_terms, code, specs=[VM, ANY],
         scratch=[pltpu.VMEM((8, HD), F32), DMA((1,))], flops=2 * 10**7, moved=10**6,
     )
-    route = ("sec", "dp")
+    route = ("dp", "sec")
     incoming = exchange(outgoing.reshape(shards, 4, HD), route).reshape(2 * slots, HD)
     slot_rows = pltpu.VMEM(incoming.shape, BF16)
-    grads, stats = call(
-        slots_kernel, (shape((2 * slots, HD)), shape((2 * group, rows), F32)),
-        incoming, stats, text_query, out_cotangent, specs=[ANY] * 4, limit=WIDE,
-        scratch=[slot_rows, pltpu.VMEM(stats.shape, F32), wide, wide, DMA((6,))],
+    grads, stats, kept = call(
+        slots_kernel, (shape((2 * slots, HD)), tall, tall_slots),
+        incoming, stats, text_query, out_cotangent, specs=[VM, ANY, ANY, ANY],
+        out_specs=(VM, ANY, ANY), limit=SLOTL,
+        scratch=[
+            pltpu.VMEM((3 * group, rows), F32), wide, wide, pltpu.VMEM((2 * group, rows), F32),
+            DMA((7,)),
+        ],
         flops=10**9, moved=2 * 10**6,
     )
     returned = exchange(grads.reshape(shards, 4, HD), route).reshape(2 * slots, HD)
     attended = call(
-        output_kernel, shape((rows, group * HD)), incoming, text_rows, stats, text_query,
-        specs=[ANY] * 4, scratch=[slot_rows, thin, pltpu.VMEM(stats.shape, F32), wide, DMA((4,))],
+        output_kernel, shape((rows, group * HD)), kept, text_rows, stats, text_query, specs=[ANY] * 4,
+        scratch=[slot_rows, thin, pltpu.VMEM((2 * group, rows), F32), wide, DMA((4,))],
         limit=WIDE, flops=10**9, moved=2 * 10**6,
     )
     returned, attended = lax.optimization_barrier((returned, attended))

time: 110 us -> 108 us (0.982)
  no operation moved by 1% of the time
where the time goes in v3:
time: 108 us
  blocking collectives  55.7 us (52%)
  Pallas kernels  21.1 us (20%)
  waiting for transfers between devices  13.3 us (12%)
  starting transfers between devices  12.4 us (11%)
  local copies, waits for them, and re-layouts  4.31 us (4%)
    all_to_all x2, blocking collectives, exchange(): return lax.all_to_all(x, axes, split_axis=0, concat_axis=0, tiled=True)  42 us
    pallas_call x9, Pallas kernels, call(): pl.pallas_call(kernel, out_shape=out_shape, in_specs=specs or [VM] * len(...  21.1 us
    all_gather x1, blocking collectives, on_device(): x = lax.all_gather(patches.T, 'mp', axis=0, tiled=True)  13.7 us
    all_to_all x3, waiting for transfers between devices, exchange(): return lax.all_to_all(x, axes, split_axis=0, concat_axis=0, tiled=True)  13.3 us
    all_to_all x3, starting transfers between devices, exchange(): return lax.all_to_all(x, axes, split_axis=0, concat_axis=0, tiled=True)  12.4 us
    reshape x1, local copies, waits for them, and re-layouts, on_device(): jnp.transpose(visual_kv.reshape(width, 2, 4, HD), (0, 2, 1, 3))  4.28 us
  transfers between devices with their start and end apart: 3, of which 3 were waited for; matrix products, arithmetic and copies ran while one was open for 4% of the time, Pallas kernels for 7%

profile of v3, /device:TPU:1, one launch (start us, length us, event | category | flops | bytes accessed | tf_op | source)
XLA Modules:
  0.0 107.5 jit_solution(9098916765135397621)
XLA Ops:
  0.6 13.7 %all_gather.3.x_hbm = bf16[1280,256]{1,0:T(8,128)(2,1)} all-gather(bf16[320,256]{1,0:T(8,128)(2,1)} %bitcast.23), channel_id=1, replica_groups=mesh['sec'=2,'dp'=64,'mp'=4] {'mp'}, dimensions={0}, use_global_device_ids=true | all-gather | bytes 819200 | tf_op jit(solution)/shard_map/all_gather | solution.py:322
  14.3 0.0 copy-start.3
  14.3 4.7 %shard_map.131 = (bf16[4,64,1280]{2,1,0:T(8,128)(2,1)}, bf16[64,1280]{1,0:T(8,128)(2,1)}) custom-call(s32[1]{0:T(128)} %bitcast.pos_ref, bf16[10,128]{1,0:T(8,128)(2,1)} %bitcast.27, s32[1,256]{1,0:T(1,128)} %bitcast.28, bf16[480,1280]{1,0:T(8,128)(2,1)} %bitcast.24, bf16[1280,256]{1,0:T(8,128)(2,1)} %all_gather.3.x_hbm, bf16[160,1280]{1,0:T(8,128)(2,1)} %proj_hbm.1), custom_call_target="tpu_custom_call" | custom-call | flops 1000000000 | bytes 4000000 | tf_op jit(solution)/shard_map/pallas_call | solution.py:37
  19.0 3.5 %all-to-all-start = ((bf16[4,64,1280]{2,1,0:T(8,128)(2,1)}), bf16[4,64,1280]{2,1,0:T(8,128)(2,1)S(1)}, u32[]{:S(2)}, u32[]{:S(2)}) async-start(bf16[4,64,1280]{2,1,0:T(8,128)(2,1)} %get-tuple-element.11), calls=%async_computation | async-start | bytes 1310720 | tf_op jit(solution)/shard_map/all_to_all | solution.py:306
  22.5 0.0 copy-done.3
  22.6 0.0 copy-start
  22.6 4.3 %reshape.52.w_ref = bf16[1280,1024]{1,0:T(8,128)(2,1)S(1)} reshape(bf16[1280,4,2,128]{3,2,1,0:T(2,128)(2,1)} %bitcast.22) | data formatting | bytes 5242880 | tf_op jit(solution)/shard_map/reshape | solution.py:339
  26.9 0.0 copy-start.1
  26.9 0.0 copy-start.2
  26.9 3.3 %all-to-all-done.in_ref = bf16[4,64,1280]{2,1,0:T(8,128)(2,1)S(1)} async-done(((bf16[4,64,1280]{2,1,0:T(8,128)(2,1)}), bf16[4,64,1280]{2,1,0:T(8,128)(2,1)S(1)}, u32[]{:S(2)}, u32[]{:S(2)}) %all-to-all-start) | async-done | bytes 655392 | tf_op jit(solution)/shard_map/all_to_all | solution.py:306
  30.1 0.0 copy-done
  30.1 1.4 %shard_map.132 = bf16[4,64,256]{2,1,0:T(8,128)(2,1)} custom-call(bf16[4,64,1280]{2,1,0:T(8,128)(2,1)S(1)} %all-to-all-done.in_ref, bf16[64,1280]{1,0:T(8,128)(2,1)S(1)} %copy-done, bf16[1,1280]{1,0:T(2,128)(2,1)S(1)} %reshape.50.gain_ref, bf16[1280,1024]{1,0:T(8,128)(2,1)S(1)} %reshape.52.w_ref), custom_call_target="tpu_custom_call" | custom-call | flops 200000000 | bytes 4000000 | tf_op jit(solution)/shard_map/pallas_call | solution.py:37
  31.5 3.3 %all-to-all-start.1 = ((bf16[4,64,256]{2,1,0:T(8,128)(2,1)}), bf16[4,64,256]{2,1,0:T(8,128)(2,1)S(1)}, u32[]{:S(2)}, u32[]{:S(2)}) async-start(bf16[4,64,256]{2,1,0:T(8,128)(2,1)} %shard_map.132), calls=%async_computation.1 | async-start | bytes 262144 | tf_op jit(solution)/shard_map/all_to_all | solution.py:306
  34.9 0.0 copy-done.1
  34.9 0.0 copy-done.2
  34.9 0.1 shard_map.134.code_hbm.code_ref
  35.0 2.8 %shard_map.133.text_hbm = f32[1024,256]{1,0:T(8,128)} custom-call(bf16[512,128]{1,0:T(8,128)(2,1)} %bitcast.25, bf16[256,1024]{1,0:T(8,128)(2,1)} %q_hbm.5, bf16[256,1024]{1,0:T(8,128)(2,1)} %c_hbm.3), custom_call_target="tpu_custom_call" | custom-call | flops 1000000000 | bytes 2000000 | tf_op jit(solution)/shard_map/pallas_call | solution.py:37
  37.8 1.8 %all-to-all-done.1.in_ref = bf16[4,64,256]{2,1,0:T(8,128)(2,1)S(1)} async-done(((bf16[4,64,256]{2,1,0:T(8,128)(2,1)}), bf16[4,64,256]{2,1,0:T(8,128)(2,1)S(1)}, u32[]{:S(2)}, u32[]{:S(2)}) %all-to-all-start.1) | async-done | bytes 131104 | tf_op jit(solution)/shard_map/all_to_all | solution.py:306
  39.7 0.2 shard_map.135
  39.9 34.8 %all_to_all.25 = bf16[128,4,128]{2,1,0:T(4,128)(2,1)S(1)} all-to-all(bf16[128,4,128]{2,1,0:T(4,128)(2,1)S(1)} %bitcast.18), channel_id=1, replica_groups=mesh['sec'=2,'dp'=64,'mp'=4] {'dp','sec'}, dimensions={0} | all-to-all | bytes 262144 | tf_op jit(solution)/shard_map/all_to_all | solution.py:306
  74.7 5.3 %shard_map.136 = (bf16[512,128]{1,0:T(8,128)(2,1)}, f32[1024,256]{1,0:T(8,128)}, bf16[4096,128]{1,0:T(8,128)(2,1)}) custom-call(bf16[512,128]{1,0:T(8,128)(2,1)S(1)} %bitcast.19, f32[1024,256]{1,0:T(8,128)} %shard_map.133.text_hbm, bf16[256,1024]{1,0:T(8,128)(2,1)} %q_hbm.5, bf16[256,1024]{1,0:T(8,128)(2,1)} %c_hbm.3), custom_call_target="tpu_custom_call" | custom-call | flops 1000000000 | bytes 2000000 | tf_op jit(solution)/shard_map/pallas_call | solution.py:37
  80.0 5.6 %all-to-all-start.3 = ((bf16[128,4,128]{2,1,0:T(4,128)(2,1)}), bf16[128,4,128]{2,1,0:T(4,128)(2,1)S(1)}, u32[]{:S(2)}, u32[]{:S(2)}) async-start(bf16[128,4,128]{2,1,0:T(4,128)(2,1)} %bitcast.13), calls=%async_computation.3 | async-start | bytes 262144 | tf_op jit(solution)/shard_map/all_to_all | solution.py:306
  85.6 4.6 %shard_map.137 = bf16[256,1024]{1,0:T(8,128)(2,1)} custom-call(bf16[4096,128]{1,0:T(8,128)(2,1)} %get-tuple-element.16.in_hbm, bf16[512,128]{1,0:T(8,128)(2,1)} %bitcast.26, f32[1024,256]{1,0:T(8,128)} %get-tuple-element.17.stats_hbm, bf16[256,1024]{1,0:T(8,128)(2,1)} %q_hbm.5), custom_call_target="tpu_custom_call" | custom-call | flops 1000000000 | bytes 2000000 | tf_op jit(solution)/shard_map/pallas_call | solution.py:37
  90.2 8.2 %all-to-all-done.3 = bf16[128,4,128]{2,1,0:T(4,128)(2,1)S(1)} async-done(((bf16[128,4,128]{2,1,0:T(4,128)(2,1)}), bf16[128,4,128]{2,1,0:T(4,128)(2,1)S(1)}, u32[]{:S(2)}, u32[]{:S(2)}) %all-to-all-start.3) | async-done | bytes 131104 | tf_op jit(solution)/shard_map/all_to_all | solution.py:306
  98.5 0.3 shard_map.138
  98.8 7.2 %all_to_all.26.in_ref = bf16[4,64,256]{2,1,0:T(8,128)(2,1)S(1)} all-to-all(bf16[4,64,256]{2,1,0:T(8,128)(2,1)S(1)} %shard_map.138), channel_id=1, replica_groups=mesh['sec'=2,'dp'=64,'mp'=4] {'mp'}, dimensions={0} | all-to-all | bytes 262144 | tf_op jit(solution)/shard_map/all_to_all | solution.py:306
  106.0 1.5 %shard_map.139 = bf16[64,1280]{1,0:T(8,128)(2,1)} custom-call(bf16[4,64,256]{2,1,0:T(8,128)(2,1)S(1)} %all_to_all.26.in_ref, bf16[1280,1024]{1,0:T(8,128)(2,1)S(1)} %reshape.52.w_ref), custom_call_target="tpu_custom_call" | custom-call | flops 200000000 | bytes 3000000 | tf_op jit(solution)/shard_map/pallas_call | solution.py:37
  (1 shorter events, 0.0 us)
Async XLA Ops:
  14.3 8.2 %copy-start.3 = (bf16[1280]{0:T(1024)(128)(2,1)S(1)}, bf16[1280]{0:T(1024)(128)(2,1)}, u32[]{:S(2)}) copy-start(bf16[1280]{0:T(1024)(128)(2,1)} %param.17) | copy-start | bytes 7684
  19.0 11.1 %all-to-all-start = ((bf16[4,64,1280]{2,1,0:T(8,128)(2,1)}), bf16[4,64,1280]{2,1,0:T(8,128)(2,1)S(1)}, u32[]{:S(2)}, u32[]{:S(2)}) async-start(bf16[4,64,1280]{2,1,0:T(8,128)(2,1)} %get-tuple-element.11), calls=%async_computation | async-start | bytes 1310720 | tf_op jit(solution)/shard_map/all_to_all | solution.py:306
  22.6 7.6 %copy-start = (bf16[64,1280]{1,0:T(8,128)(2,1)S(1)}, bf16[64,1280]{1,0:T(8,128)(2,1)}, u32[]{:S(2)}) copy-start(bf16[64,1280]{1,0:T(8,128)(2,1)} %get-tuple-element.12.own_ref) | copy-start | bytes 491524
  26.9 8.0 %copy-start.1 = (s32[64]{0:T(128)S(1)}, s32[64]{0:T(128)}, u32[]{:S(2)}) copy-start(s32[64]{0:T(128)} %param.18) | copy-start | bytes 772
  26.9 8.0 %copy-start.2 = (s32[64]{0:T(128)S(1)}, s32[64]{0:T(128)}, u32[]{:S(2)}) copy-start(s32[64]{0:T(128)} %param.19) | copy-start | bytes 772
  31.5 8.1 %all-to-all-start.1 = ((bf16[4,64,256]{2,1,0:T(8,128)(2,1)}), bf16[4,64,256]{2,1,0:T(8,128)(2,1)S(1)}, u32[]{:S(2)}, u32[]{:S(2)}) async-start(bf16[4,64,256]{2,1,0:T(8,128)(2,1)} %shard_map.132), calls=%async_computation.1 | async-start | bytes 262144 | tf_op jit(solution)/shard_map/all_to_all | solution.py:306
  80.0 18.4 %all-to-all-start.3 = ((bf16[128,4,128]{2,1,0:T(4,128)(2,1)}), bf16[128,4,128]{2,1,0:T(4,128)(2,1)S(1)}, u32[]{:S(2)}, u32[]{:S(2)}) async-start(bf16[128,4,128]{2,1,0:T(4,128)(2,1)} %bitcast.13), calls=%async_computation.3 | async-start | bytes 262144 | tf_op jit(solution)/shard_map/all_to_all | solution.py:306

commit v4 on v3

--- a/solution.py
+++ b/solution.py
@@ -228,6 +228,7 @@
     stats.wait()
     dk = jnp.zeros((slots, HD), F32)
     dv = jnp.zeros((slots, HD), F32)
+    held = [[], [], [], []]
     for g in range(group):
         if g % (group // 2) == 0:
             for copy in copies[:2] if g == 0 else copies[2:]:
@@ -247,9 +248,15 @@
         stats_ref[g : g + 1] = m
         stats_ref[group + g : group + g + 1] = inv
         p = e * inv
-        ds = (p * (dp - delta)).astype(BF16)
-        dk = dk + dot(ds, q)
-        dv = dv + dot(p.astype(BF16), c)
+        lists = ((p * (dp - delta)).astype(BF16), p.astype(BF16), q, c)
+        for some, one in zip(held, lists):
+            some.append(one)
+        if g % (group // 2) == group // 2 - 1:
+            ds, ps = (jnp.concatenate(some, axis=1) for some in held[:2])
+            qs, cs = (jnp.concatenate(some, axis=0) for some in held[2:])
+            dk = dk + dot(ds, qs)
+            dv = dv + dot(ps, cs)
+            held = [[], [], [], []]
     sent = fetch([(stats_ref, head_of(stats_hbm, stats_ref))], sems.at[pl.ds(5, 1)])[0]
     dk = (dk * (1.0 / math.sqrt(HD))).astype(BF16)
     dv = dv.astype(BF16)
@@ -272,17 +279,16 @@
     rows = q_ref.shape[0]
     kt, vt = text_pair(kv_ref)
     ks, vs, bias = slot_pair(in_ref)
-    vt = vt.T
-    vs = vs.T
+    values = jnp.concatenate([vt, vs], axis=0).T
     causal = iota((rows, rows), 0) <= iota((rows, rows), 1)
     for g in range(group):
         qt = q_ref[:, g * HD : (g + 1) * HD].T
         m = stats_ref[g : g + 1]
         inv = stats_ref[group + g : group + g + 1]
-        s = jnp.where(causal, dot(kt, qt) * SCALE2, NEG)
-        o = dot(vt, (jnp.exp2(s - m) * inv).astype(BF16))
-        s = dot(ks, qt) * SCALE2 + bias
-        o = o + dot(vs, (jnp.exp2(s - m) * inv).astype(BF16))
+        text = jnp.where(causal, dot(kt, qt) * SCALE2, NEG)
+        slot = dot(ks, qt) * SCALE2 + bias
+        s = jnp.concatenate([text, slot], axis=0)
+        o = dot(values, (jnp.exp2(s - m) * inv).astype(BF16))
         out_ref[:, g * HD : (g + 1) * HD] = o.T.astype(BF16)
 
 

time: 108 us -> 107 us (level)
  Pallas kernels: 21.1 us -> 19.5 us
    pallas_call x9, Pallas kernels: 21.1 us -> 19.5 us  [call(): pl.pallas_call(kernel, out_shape=out_shape, in_specs=specs or [VM] * len(...]
where the time goes in v4:
time: 107 us; the launch traced here: 106 us
  blocking collectives  55.7 us (52%)
  Pallas kernels  19.5 us (18%)
  waiting for transfers between devices  13.6 us (13%)
  starting transfers between devices  12.4 us (12%)
  local copies, waits for them, and re-layouts  4.31 us (4%)
    all_to_all x2, blocking collectives, exchange(): return lax.all_to_all(x, axes, split_axis=0, concat_axis=0, tiled=True)  42 us
    pallas_call x9, Pallas kernels, call(): pl.pallas_call(kernel, out_shape=out_shape, in_specs=specs or [VM] * len(...  19.5 us
    all_gather x1, blocking collectives, on_device(): x = lax.all_gather(patches.T, 'mp', axis=0, tiled=True)  13.7 us
    all_to_all x3, waiting for transfers between devices, exchange(): return lax.all_to_all(x, axes, split_axis=0, concat_axis=0, tiled=True)  13.6 us
    all_to_all x3, starting transfers between devices, exchange(): return lax.all_to_all(x, axes, split_axis=0, concat_axis=0, tiled=True)  12.4 us
    reshape x1, local copies, waits for them, and re-layouts, on_device(): jnp.transpose(visual_kv.reshape(width, 2, 4, HD), (0, 2, 1, 3))  4.28 us
  transfers between devices with their start and end apart: 3, of which 3 were waited for; matrix products, arithmetic and copies ran while one was open for 4% of the time, Pallas kernels for 7%

profile of v4, /device:TPU:1, one launch (start us, length us, event | category | flops | bytes accessed | tf_op | source)
XLA Modules:
  0.0 106.3 jit_solution(5896748676747223882)
XLA Ops:
  0.6 13.7 %all_gather.3.x_hbm = bf16[1280,256]{1,0:T(8,128)(2,1)} all-gather(bf16[320,256]{1,0:T(8,128)(2,1)} %bitcast.23), channel_id=1, replica_groups=mesh['sec'=2,'dp'=64,'mp'=4] {'mp'}, dimensions={0}, use_global_device_ids=true | all-gather | bytes 819200 | tf_op jit(solution)/shard_map/all_gather | solution.py:328
  14.3 0.0 copy-start.3
  14.3 4.7 %shard_map.131 = (bf16[4,64,1280]{2,1,0:T(8,128)(2,1)}, bf16[64,1280]{1,0:T(8,128)(2,1)}) custom-call(s32[1]{0:T(128)} %bitcast.pos_ref, bf16[10,128]{1,0:T(8,128)(2,1)} %bitcast.27, s32[1,256]{1,0:T(1,128)} %bitcast.28, bf16[480,1280]{1,0:T(8,128)(2,1)} %bitcast.24, bf16[1280,256]{1,0:T(8,128)(2,1)} %all_gather.3.x_hbm, bf16[160,1280]{1,0:T(8,128)(2,1)} %proj_hbm.1), custom_call_target="tpu_custom_call" | custom-call | flops 1000000000 | bytes 4000000 | tf_op jit(solution)/shard_map/pallas_call | solution.py:37
  19.0 3.5 %all-to-all-start = ((bf16[4,64,1280]{2,1,0:T(8,128)(2,1)}), bf16[4,64,1280]{2,1,0:T(8,128)(2,1)S(1)}, u32[]{:S(2)}, u32[]{:S(2)}) async-start(bf16[4,64,1280]{2,1,0:T(8,128)(2,1)} %get-tuple-element.11), calls=%async_computation | async-start | bytes 1310720 | tf_op jit(solution)/shard_map/all_to_all | solution.py:312
  22.5 0.0 copy-done.3
  22.6 0.0 copy-start
  22.6 4.3 %reshape.52.w_ref = bf16[1280,1024]{1,0:T(8,128)(2,1)S(1)} reshape(bf16[1280,4,2,128]{3,2,1,0:T(2,128)(2,1)} %bitcast.22) | data formatting | bytes 5242880 | tf_op jit(solution)/shard_map/reshape | solution.py:345
  26.9 0.0 copy-start.1
  26.9 0.0 copy-start.2
  26.9 3.3 %all-to-all-done.in_ref = bf16[4,64,1280]{2,1,0:T(8,128)(2,1)S(1)} async-done(((bf16[4,64,1280]{2,1,0:T(8,128)(2,1)}), bf16[4,64,1280]{2,1,0:T(8,128)(2,1)S(1)}, u32[]{:S(2)}, u32[]{:S(2)}) %all-to-all-start) | async-done | bytes 655392 | tf_op jit(solution)/shard_map/all_to_all | solution.py:312
  30.1 0.0 copy-done
  30.1 1.4 %shard_map.132 = bf16[4,64,256]{2,1,0:T(8,128)(2,1)} custom-call(bf16[4,64,1280]{2,1,0:T(8,128)(2,1)S(1)} %all-to-all-done.in_ref, bf16[64,1280]{1,0:T(8,128)(2,1)S(1)} %copy-done, bf16[1,1280]{1,0:T(2,128)(2,1)S(1)} %reshape.50.gain_ref, bf16[1280,1024]{1,0:T(8,128)(2,1)S(1)} %reshape.52.w_ref), custom_call_target="tpu_custom_call" | custom-call | flops 200000000 | bytes 4000000 | tf_op jit(solution)/shard_map/pallas_call | solution.py:37
  31.5 3.3 %all-to-all-start.1 = ((bf16[4,64,256]{2,1,0:T(8,128)(2,1)}), bf16[4,64,256]{2,1,0:T(8,128)(2,1)S(1)}, u32[]{:S(2)}, u32[]{:S(2)}) async-start(bf16[4,64,256]{2,1,0:T(8,128)(2,1)} %shard_map.132), calls=%async_computation.1 | async-start | bytes 262144 | tf_op jit(solution)/shard_map/all_to_all | solution.py:312
  34.9 0.0 copy-done.1
  34.9 0.0 copy-done.2
  34.9 0.1 shard_map.134.code_hbm.code_ref
  35.0 2.8 %shard_map.133.text_hbm = f32[1024,256]{1,0:T(8,128)} custom-call(bf16[512,128]{1,0:T(8,128)(2,1)} %bitcast.25, bf16[256,1024]{1,0:T(8,128)(2,1)} %q_hbm.5, bf16[256,1024]{1,0:T(8,128)(2,1)} %c_hbm.3), custom_call_target="tpu_custom_call" | custom-call | flops 1000000000 | bytes 2000000 | tf_op jit(solution)/shard_map/pallas_call | solution.py:37
  37.8 1.8 %all-to-all-done.1.in_ref = bf16[4,64,256]{2,1,0:T(8,128)(2,1)S(1)} async-done(((bf16[4,64,256]{2,1,0:T(8,128)(2,1)}), bf16[4,64,256]{2,1,0:T(8,128)(2,1)S(1)}, u32[]{:S(2)}, u32[]{:S(2)}) %all-to-all-start.1) | async-done | bytes 131104 | tf_op jit(solution)/shard_map/all_to_all | solution.py:312
  39.7 0.2 shard_map.135
  39.9 34.8 %all_to_all.25 = bf16[128,4,128]{2,1,0:T(4,128)(2,1)S(1)} all-to-all(bf16[128,4,128]{2,1,0:T(4,128)(2,1)S(1)} %bitcast.18), channel_id=1, replica_groups=mesh['sec'=2,'dp'=64,'mp'=4] {'dp','sec'}, dimensions={0} | all-to-all | bytes 262144 | tf_op jit(solution)/shard_map/all_to_all | solution.py:312
  74.7 4.1 %shard_map.136 = (bf16[512,128]{1,0:T(8,128)(2,1)}, f32[1024,256]{1,0:T(8,128)}, bf16[4096,128]{1,0:T(8,128)(2,1)}) custom-call(bf16[512,128]{1,0:T(8,128)(2,1)S(1)} %bitcast.19, f32[1024,256]{1,0:T(8,128)} %shard_map.133.text_hbm, bf16[256,1024]{1,0:T(8,128)(2,1)} %q_hbm.5, bf16[256,1024]{1,0:T(8,128)(2,1)} %c_hbm.3), custom_call_target="tpu_custom_call" | custom-call | flops 1000000000 | bytes 2000000 | tf_op jit(solution)/shard_map/pallas_call | solution.py:37
  78.8 5.6 %all-to-all-start.3 = ((bf16[128,4,128]{2,1,0:T(4,128)(2,1)}), bf16[128,4,128]{2,1,0:T(4,128)(2,1)S(1)}, u32[]{:S(2)}, u32[]{:S(2)}) async-start(bf16[128,4,128]{2,1,0:T(4,128)(2,1)} %bitcast.13), calls=%async_computation.3 | async-start | bytes 262144 | tf_op jit(solution)/shard_map/all_to_all | solution.py:312
  84.4 4.3 %shard_map.137 = bf16[256,1024]{1,0:T(8,128)(2,1)} custom-call(bf16[4096,128]{1,0:T(8,128)(2,1)} %get-tuple-element.16.in_hbm, bf16[512,128]{1,0:T(8,128)(2,1)} %bitcast.26, f32[1024,256]{1,0:T(8,128)} %get-tuple-element.17.stats_hbm, bf16[256,1024]{1,0:T(8,128)(2,1)} %q_hbm.5), custom_call_target="tpu_custom_call" | custom-call | flops 1000000000 | bytes 2000000 | tf_op jit(solution)/shard_map/pallas_call | solution.py:37
  88.7 8.5 %all-to-all-done.3 = bf16[128,4,128]{2,1,0:T(4,128)(2,1)S(1)} async-done(((bf16[128,4,128]{2,1,0:T(4,128)(2,1)}), bf16[128,4,128]{2,1,0:T(4,128)(2,1)S(1)}, u32[]{:S(2)}, u32[]{:S(2)}) %all-to-all-start.3) | async-done | bytes 131104 | tf_op jit(solution)/shard_map/all_to_all | solution.py:312
  97.2 0.3 shard_map.138
  97.5 7.2 %all_to_all.26.in_ref = bf16[4,64,256]{2,1,0:T(8,128)(2,1)S(1)} all-to-all(bf16[4,64,256]{2,1,0:T(8,128)(2,1)S(1)} %shard_map.138), channel_id=1, replica_groups=mesh['sec'=2,'dp'=64,'mp'=4] {'mp'}, dimensions={0} | all-to-all | bytes 262144 | tf_op jit(solution)/shard_map/all_to_all | solution.py:312
  104.8 1.5 %shard_map.139 = bf16[64,1280]{1,0:T(8,128)(2,1)} custom-call(bf16[4,64,256]{2,1,0:T(8,128)(2,1)S(1)} %all_to_all.26.in_ref, bf16[1280,1024]{1,0:T(8,128)(2,1)S(1)} %reshape.52.w_ref), custom_call_target="tpu_custom_call" | custom-call | flops 200000000 | bytes 3000000 | tf_op jit(solution)/shard_map/pallas_call | solution.py:37
  (1 shorter events, 0.0 us)
Async XLA Ops:
  14.3 8.2 %copy-start.3 = (bf16[1280]{0:T(1024)(128)(2,1)S(1)}, bf16[1280]{0:T(1024)(128)(2,1)}, u32[]{:S(2)}) copy-start(bf16[1280]{0:T(1024)(128)(2,1)} %param.17) | copy-start | bytes 7684
  19.0 11.1 %all-to-all-start = ((bf16[4,64,1280]{2,1,0:T(8,128)(2,1)}), bf16[4,64,1280]{2,1,0:T(8,128)(2,1)S(1)}, u32[]{:S(2)}, u32[]{:S(2)}) async-start(bf16[4,64,1280]{2,1,0:T(8,128)(2,1)} %get-tuple-element.11), calls=%async_computation | async-start | bytes 1310720 | tf_op jit(solution)/shard_map/all_to_all | solution.py:312
  22.6 7.6 %copy-start = (bf16[64,1280]{1,0:T(8,128)(2,1)S(1)}, bf16[64,1280]{1,0:T(8,128)(2,1)}, u32[]{:S(2)}) copy-start(bf16[64,1280]{1,0:T(8,128)(2,1)} %get-tuple-element.12.own_ref) | copy-start | bytes 491524
  26.9 8.0 %copy-start.1 = (s32[64]{0:T(128)S(1)}, s32[64]{0:T(128)}, u32[]{:S(2)}) copy-start(s32[64]{0:T(128)} %param.18) | copy-start | bytes 772
  26.9 8.0 %copy-start.2 = (s32[64]{0:T(128)S(1)}, s32[64]{0:T(128)}, u32[]{:S(2)}) copy-start(s32[64]{0:T(128)} %param.19) | copy-start | bytes 772
  31.5 8.1 %all-to-all-start.1 = ((bf16[4,64,256]{2,1,0:T(8,128)(2,1)}), bf16[4,64,256]{2,1,0:T(8,128)(2,1)S(1)}, u32[]{:S(2)}, u32[]{:S(2)}) async-start(bf16[4,64,256]{2,1,0:T(8,128)(2,1)} %shard_map.132), calls=%async_computation.1 | async-start | bytes 262144 | tf_op jit(solution)/shard_map/all_to_all | solution.py:312
  78.8 18.4 %all-to-all-start.3 = ((bf16[128,4,128]{2,1,0:T(4,128)(2,1)}), bf16[128,4,128]{2,1,0:T(4,128)(2,1)S(1)}, u32[]{:S(2)}, u32[]{:S(2)}) async-start(bf16[128,4,128]{2,1,0:T(4,128)(2,1)} %bitcast.13), calls=%async_computation.3 | async-start | bytes 262144 | tf_op jit(solution)/shard_map/all_to_all | solution.py:312

commit v5 on v4

--- a/solution.py
+++ b/solution.py
@@ -152,28 +152,17 @@
     return tall.at[pl.ds(0, ref.shape[0])]
 
 
-def halves(ref):
-    half = ref.shape[1] // 2
-    return [ref.at[:, :half], ref.at[:, half:]]
-
-
-def fetch_wide(q_hbm, c_hbm, q_ref, c_ref, sems):
-    pairs = list(zip(halves(q_hbm) + halves(c_hbm), halves(q_ref) + halves(c_ref)))
-    q0, q1, c0, c1 = pairs
-    return fetch([q0, c0, q1, c1], sems)
-
-
 def text_kernel(kv_hbm, q_hbm, c_hbm, stats_hbm, kv_ref, q_ref, c_ref, stats_ref, sems):
     head = fetch([(kv_hbm, kv_ref)], sems.at[pl.ds(0, 1)])[0]
-    copies = fetch_wide(q_hbm, c_hbm, q_ref, c_ref, sems.at[pl.ds(1, 4)])
+    copies = fetch([(q_hbm, q_ref), (c_hbm, c_ref)], sems.at[pl.ds(1, 2)])
     group = q_ref.shape[1] // HD
     rows = q_ref.shape[0]
     head.wait()
     k, v = text_pair(kv_ref)
     causal = iota((rows, rows), 0) <= iota((rows, rows), 1)
     for g in range(group):
-        if g % (group // 2) == 0:
-            for copy in copies[:2] if g == 0 else copies[2:]:
+        if g == 0:
+            for copy in copies:
                 copy.wait()
         s = jnp.where(causal, dot(k, q_ref[:, g * HD : (g + 1) * HD].T) * SCALE2, NEG)
         m = jnp.max(s, axis=0, keepdims=True)
@@ -182,7 +171,7 @@
         stats_ref[g : g + 1] = m
         stats_ref[group + g : group + g + 1] = jnp.sum(e, axis=0, keepdims=True)
         stats_ref[2 * group + g : 2 * group + g + 1] = jnp.sum(e * dp, axis=0, keepdims=True)
-    fetch([(stats_ref, head_of(stats_hbm, stats_ref))], sems.at[pl.ds(5, 1)])[0].wait()
+    fetch([(stats_ref, head_of(stats_hbm, stats_ref))], sems.at[pl.ds(3, 1)])[0].wait()
 
 
 def text_pair(kv_ref):
@@ -218,10 +207,10 @@
     in_ref, text_hbm, q_hbm, c_hbm, out_ref, stats_hbm, in_hbm,
     text_ref, q_ref, c_ref, stats_ref, sems,
 ):
-    copies = fetch_wide(q_hbm, c_hbm, q_ref, c_ref, sems.at[pl.ds(1, 4)])
+    copies = fetch([(q_hbm, q_ref), (c_hbm, c_ref)], sems.at[pl.ds(1, 2)])
     pairs = [(head_of(text_hbm, text_ref), text_ref)]
     stats = fetch(pairs, sems.at[pl.ds(0, 1)])[0]
-    kept = fetch([(in_ref, head_of(in_hbm, in_ref))], sems.at[pl.ds(6, 1)])[0]
+    kept = fetch([(in_ref, head_of(in_hbm, in_ref))], sems.at[pl.ds(4, 1)])[0]
     group = q_ref.shape[1] // HD
     k, v, bias = slot_pair(in_ref)
     slots = k.shape[0]
@@ -230,8 +219,8 @@
     dv = jnp.zeros((slots, HD), F32)
     held = [[], [], [], []]
     for g in range(group):
-        if g % (group // 2) == 0:
-            for copy in copies[:2] if g == 0 else copies[2:]:
+        if g == 0:
+            for copy in copies:
                 copy.wait()
         q = q_ref[:, g * HD : (g + 1) * HD]
         c = c_ref[:, g * HD : (g + 1) * HD]
@@ -257,7 +246,7 @@
             dk = dk + dot(ds, qs)
             dv = dv + dot(ps, cs)
             held = [[], [], [], []]
-    sent = fetch([(stats_ref, head_of(stats_hbm, stats_ref))], sems.at[pl.ds(5, 1)])[0]
+    sent = fetch([(stats_ref, head_of(stats_hbm, stats_ref))], sems.at[pl.ds(3, 1)])[0]
     dk = (dk * (1.0 / math.sqrt(HD))).astype(BF16)
     dv = dv.astype(BF16)
     order = one_hot(iota((HD, HD), 0) == slot_place(iota((HD, HD), 1)))
@@ -357,7 +346,7 @@
     stats = call(
         text_kernel, tall, text_rows, text_query, out_cotangent,
         specs=[ANY] * 3, out_specs=ANY,
-        scratch=[thin, wide, wide, pltpu.VMEM((3 * group, rows), F32), DMA((6,))], limit=WIDE,
+        scratch=[thin, wide, wide, pltpu.VMEM((3 * group, rows), F32), DMA((4,))], limit=WIDE,
         flops=10**9, moved=2 * 10**6,
     )
     kv_terms, stats = lax.optimization_barrier((kv_terms, stats))
@@ -374,7 +363,7 @@
         out_specs=(VM, ANY, ANY), limit=SLOTL,
         scratch=[
             pltpu.VMEM((3 * group, rows), F32), wide, wide, pltpu.VMEM((2 * group, rows), F32),
-            DMA((7,)),
+            DMA((5,)),
         ],
         flops=10**9, moved=2 * 10**6,
     )

time: 107 us -> 107 us (level)
  no operation moved by 1% of the time
where the time goes in v5:
time: 107 us; the launch traced here: 106 us
  blocking collectives  55.7 us (52%)
  Pallas kernels  19.4 us (18%)
  waiting for transfers between devices  13.6 us (13%)
  starting transfers between devices  12.4 us (12%)
  local copies, waits for them, and re-layouts  4.31 us (4%)
    all_to_all x2, blocking collectives, exchange(): return lax.all_to_all(x, axes, split_axis=0, concat_axis=0, tiled=True)  42 us
    pallas_call x9, Pallas kernels, call(): pl.pallas_call(kernel, out_shape=out_shape, in_specs=specs or [VM] * len(...  19.4 us
    all_gather x1, blocking collectives, on_device(): x = lax.all_gather(patches.T, 'mp', axis=0, tiled=True)  13.7 us
    all_to_all x3, waiting for transfers between devices, exchange(): return lax.all_to_all(x, axes, split_axis=0, concat_axis=0, tiled=True)  13.6 us
    all_to_all x3, starting transfers between devices, exchange(): return lax.all_to_all(x, axes, split_axis=0, concat_axis=0, tiled=True)  12.4 us
    reshape x1, local copies, waits for them, and re-layouts, on_device(): jnp.transpose(visual_kv.reshape(width, 2, 4, HD), (0, 2, 1, 3))  4.28 us
  transfers between devices with their start and end apart: 3, of which 3 were waited for; matrix products, arithmetic and copies ran while one was open for 4% of the time, Pallas kernels for 7%

profile of v5, /device:TPU:1, one launch (start us, length us, event | category | flops | bytes accessed | tf_op | source)
XLA Modules:
  0.0 106.2 jit_solution(4357551117549029297)
XLA Ops:
  0.6 13.7 %all_gather.3.x_hbm = bf16[1280,256]{1,0:T(8,128)(2,1)} all-gather(bf16[320,256]{1,0:T(8,128)(2,1)} %bitcast.23), channel_id=1, replica_groups=mesh['sec'=2,'dp'=64,'mp'=4] {'mp'}, dimensions={0}, use_global_device_ids=true | all-gather | bytes 819200 | tf_op jit(solution)/shard_map/all_gather | solution.py:317
  14.3 0.0 copy-start.3
  14.3 4.7 %shard_map.131 = (bf16[4,64,1280]{2,1,0:T(8,128)(2,1)}, bf16[64,1280]{1,0:T(8,128)(2,1)}) custom-call(s32[1]{0:T(128)} %bitcast.pos_ref, bf16[10,128]{1,0:T(8,128)(2,1)} %bitcast.27, s32[1,256]{1,0:T(1,128)} %bitcast.28, bf16[480,1280]{1,0:T(8,128)(2,1)} %bitcast.24, bf16[1280,256]{1,0:T(8,128)(2,1)} %all_gather.3.x_hbm, bf16[160,1280]{1,0:T(8,128)(2,1)} %proj_hbm.1), custom_call_target="tpu_custom_call" | custom-call | flops 1000000000 | bytes 4000000 | tf_op jit(solution)/shard_map/pallas_call | solution.py:37
  19.0 3.5 %all-to-all-start = ((bf16[4,64,1280]{2,1,0:T(8,128)(2,1)}), bf16[4,64,1280]{2,1,0:T(8,128)(2,1)S(1)}, u32[]{:S(2)}, u32[]{:S(2)}) async-start(bf16[4,64,1280]{2,1,0:T(8,128)(2,1)} %get-tuple-element.11), calls=%async_computation | async-start | bytes 1310720 | tf_op jit(solution)/shard_map/all_to_all | solution.py:301
  22.5 0.0 copy-done.3
  22.6 0.0 copy-start
  22.6 4.3 %reshape.52.w_ref = bf16[1280,1024]{1,0:T(8,128)(2,1)S(1)} reshape(bf16[1280,4,2,128]{3,2,1,0:T(2,128)(2,1)} %bitcast.22) | data formatting | bytes 5242880 | tf_op jit(solution)/shard_map/reshape | solution.py:334
  26.9 0.0 copy-start.1
  26.9 0.0 copy-start.2
  26.9 3.3 %all-to-all-done.in_ref = bf16[4,64,1280]{2,1,0:T(8,128)(2,1)S(1)} async-done(((bf16[4,64,1280]{2,1,0:T(8,128)(2,1)}), bf16[4,64,1280]{2,1,0:T(8,128)(2,1)S(1)}, u32[]{:S(2)}, u32[]{:S(2)}) %all-to-all-start) | async-done | bytes 655392 | tf_op jit(solution)/shard_map/all_to_all | solution.py:301
  30.1 0.0 copy-done
  30.1 1.4 %shard_map.132 = bf16[4,64,256]{2,1,0:T(8,128)(2,1)} custom-call(bf16[4,64,1280]{2,1,0:T(8,128)(2,1)S(1)} %all-to-all-done.in_ref, bf16[64,1280]{1,0:T(8,128)(2,1)S(1)} %copy-done, bf16[1,1280]{1,0:T(2,128)(2,1)S(1)} %reshape.50.gain_ref, bf16[1280,1024]{1,0:T(8,128)(2,1)S(1)} %reshape.52.w_ref), custom_call_target="tpu_custom_call" | custom-call | flops 200000000 | bytes 4000000 | tf_op jit(solution)/shard_map/pallas_call | solution.py:37
  31.5 3.3 %all-to-all-start.1 = ((bf16[4,64,256]{2,1,0:T(8,128)(2,1)}), bf16[4,64,256]{2,1,0:T(8,128)(2,1)S(1)}, u32[]{:S(2)}, u32[]{:S(2)}) async-start(bf16[4,64,256]{2,1,0:T(8,128)(2,1)} %shard_map.132), calls=%async_computation.1 | async-start | bytes 262144 | tf_op jit(solution)/shard_map/all_to_all | solution.py:301
  34.9 0.0 copy-done.1
  34.9 0.0 copy-done.2
  34.9 0.1 shard_map.134.code_hbm.code_ref
  35.0 2.8 %shard_map.133.text_hbm = f32[1024,256]{1,0:T(8,128)} custom-call(bf16[512,128]{1,0:T(8,128)(2,1)} %bitcast.25, bf16[256,1024]{1,0:T(8,128)(2,1)} %q_hbm.5, bf16[256,1024]{1,0:T(8,128)(2,1)} %c_hbm.3), custom_call_target="tpu_custom_call" | custom-call | flops 1000000000 | bytes 2000000 | tf_op jit(solution)/shard_map/pallas_call | solution.py:37
  37.8 1.9 %all-to-all-done.1.in_ref = bf16[4,64,256]{2,1,0:T(8,128)(2,1)S(1)} async-done(((bf16[4,64,256]{2,1,0:T(8,128)(2,1)}), bf16[4,64,256]{2,1,0:T(8,128)(2,1)S(1)}, u32[]{:S(2)}, u32[]{:S(2)}) %all-to-all-start.1) | async-done | bytes 131104 | tf_op jit(solution)/shard_map/all_to_all | solution.py:301
  39.7 0.2 shard_map.135
  39.9 34.8 %all_to_all.25 = bf16[128,4,128]{2,1,0:T(4,128)(2,1)S(1)} all-to-all(bf16[128,4,128]{2,1,0:T(4,128)(2,1)S(1)} %bitcast.18), channel_id=1, replica_groups=mesh['sec'=2,'dp'=64,'mp'=4] {'dp','sec'}, dimensions={0} | all-to-all | bytes 262144 | tf_op jit(solution)/shard_map/all_to_all | solution.py:301
  74.7 4.0 %shard_map.136 = (bf16[512,128]{1,0:T(8,128)(2,1)}, f32[1024,256]{1,0:T(8,128)}, bf16[4096,128]{1,0:T(8,128)(2,1)}) custom-call(bf16[512,128]{1,0:T(8,128)(2,1)S(1)} %bitcast.19, f32[1024,256]{1,0:T(8,128)} %shard_map.133.text_hbm, bf16[256,1024]{1,0:T(8,128)(2,1)} %q_hbm.5, bf16[256,1024]{1,0:T(8,128)(2,1)} %c_hbm.3), custom_call_target="tpu_custom_call" | custom-call | flops 1000000000 | bytes 2000000 | tf_op jit(solution)/shard_map/pallas_call | solution.py:37
  78.7 5.6 %all-to-all-start.3 = ((bf16[128,4,128]{2,1,0:T(4,128)(2,1)}), bf16[128,4,128]{2,1,0:T(4,128)(2,1)S(1)}, u32[]{:S(2)}, u32[]{:S(2)}) async-start(bf16[128,4,128]{2,1,0:T(4,128)(2,1)} %bitcast.13), calls=%async_computation.3 | async-start | bytes 262144 | tf_op jit(solution)/shard_map/all_to_all | solution.py:301
  84.3 4.3 %shard_map.137 = bf16[256,1024]{1,0:T(8,128)(2,1)} custom-call(bf16[4096,128]{1,0:T(8,128)(2,1)} %get-tuple-element.16.in_hbm, bf16[512,128]{1,0:T(8,128)(2,1)} %bitcast.26, f32[1024,256]{1,0:T(8,128)} %get-tuple-element.17.stats_hbm, bf16[256,1024]{1,0:T(8,128)(2,1)} %q_hbm.5), custom_call_target="tpu_custom_call" | custom-call | flops 1000000000 | bytes 2000000 | tf_op jit(solution)/shard_map/pallas_call | solution.py:37
  88.6 8.5 %all-to-all-done.3 = bf16[128,4,128]{2,1,0:T(4,128)(2,1)S(1)} async-done(((bf16[128,4,128]{2,1,0:T(4,128)(2,1)}), bf16[128,4,128]{2,1,0:T(4,128)(2,1)S(1)}, u32[]{:S(2)}, u32[]{:S(2)}) %all-to-all-start.3) | async-done | bytes 131104 | tf_op jit(solution)/shard_map/all_to_all | solution.py:301
  97.1 0.3 shard_map.138
  97.4 7.2 %all_to_all.26.in_ref = bf16[4,64,256]{2,1,0:T(8,128)(2,1)S(1)} all-to-all(bf16[4,64,256]{2,1,0:T(8,128)(2,1)S(1)} %shard_map.138), channel_id=1, replica_groups=mesh['sec'=2,'dp'=64,'mp'=4] {'mp'}, dimensions={0} | all-to-all | bytes 262144 | tf_op jit(solution)/shard_map/all_to_all | solution.py:301
  104.7 1.5 %shard_map.139 = bf16[64,1280]{1,0:T(8,128)(2,1)} custom-call(bf16[4,64,256]{2,1,0:T(8,128)(2,1)S(1)} %all_to_all.26.in_ref, bf16[1280,1024]{1,0:T(8,128)(2,1)S(1)} %reshape.52.w_ref), custom_call_target="tpu_custom_call" | custom-call | flops 200000000 | bytes 3000000 | tf_op jit(solution)/shard_map/pallas_call | solution.py:37
  (1 shorter events, 0.0 us)
Async XLA Ops:
  14.3 8.2 %copy-start.3 = (bf16[1280]{0:T(1024)(128)(2,1)S(1)}, bf16[1280]{0:T(1024)(128)(2,1)}, u32[]{:S(2)}) copy-start(bf16[1280]{0:T(1024)(128)(2,1)} %param.17) | copy-start | bytes 7684
  19.0 11.1 %all-to-all-start = ((bf16[4,64,1280]{2,1,0:T(8,128)(2,1)}), bf16[4,64,1280]{2,1,0:T(8,128)(2,1)S(1)}, u32[]{:S(2)}, u32[]{:S(2)}) async-start(bf16[4,64,1280]{2,1,0:T(8,128)(2,1)} %get-tuple-element.11), calls=%async_computation | async-start | bytes 1310720 | tf_op jit(solution)/shard_map/all_to_all | solution.py:301
  22.6 7.6 %copy-start = (bf16[64,1280]{1,0:T(8,128)(2,1)S(1)}, bf16[64,1280]{1,0:T(8,128)(2,1)}, u32[]{:S(2)}) copy-start(bf16[64,1280]{1,0:T(8,128)(2,1)} %get-tuple-element.12.own_ref) | copy-start | bytes 491524
  26.9 8.0 %copy-start.1 = (s32[64]{0:T(128)S(1)}, s32[64]{0:T(128)}, u32[]{:S(2)}) copy-start(s32[64]{0:T(128)} %param.18) | copy-start | bytes 772
  26.9 8.0 %copy-start.2 = (s32[64]{0:T(128)S(1)}, s32[64]{0:T(128)}, u32[]{:S(2)}) copy-start(s32[64]{0:T(128)} %param.19) | copy-start | bytes 772
  31.5 8.1 %all-to-all-start.1 = ((bf16[4,64,256]{2,1,0:T(8,128)(2,1)}), bf16[4,64,256]{2,1,0:T(8,128)(2,1)S(1)}, u32[]{:S(2)}, u32[]{:S(2)}) async-start(bf16[4,64,256]{2,1,0:T(8,128)(2,1)} %shard_map.132), calls=%async_computation.1 | async-start | bytes 262144 | tf_op jit(solution)/shard_map/all_to_all | solution.py:301
  78.7 18.4 %all-to-all-start.3 = ((bf16[128,4,128]{2,1,0:T(4,128)(2,1)}), bf16[128,4,128]{2,1,0:T(4,128)(2,1)S(1)}, u32[]{:S(2)}, u32[]{:S(2)}) async-start(bf16[128,4,128]{2,1,0:T(4,128)(2,1)} %bitcast.13), calls=%async_computation.3 | async-start | bytes 262144 | tf_op jit(solution)/shard_map/all_to_all | solution.py:301

commit v6 on v5

--- a/solution.py
+++ b/solution.py
@@ -260,14 +260,17 @@
 def output_kernel(
     in_hbm, kv_hbm, stats_hbm, q_hbm, out_ref, in_ref, kv_ref, stats_ref, q_ref, sems
 ):
-    pairs = [(head_of(in_hbm, in_ref), in_ref), (kv_hbm, kv_ref), (q_hbm, q_ref)]
+    pairs = [(kv_hbm, kv_ref), (head_of(in_hbm, in_ref), in_ref), (q_hbm, q_ref)]
     pairs += [(head_of(stats_hbm, stats_ref), stats_ref)]
-    for copy in fetch(pairs, sems):
-        copy.wait()
+    copies = fetch(pairs, sems)
     group = q_ref.shape[1] // HD
     rows = q_ref.shape[0]
+    copies[0].wait()
     kt, vt = text_pair(kv_ref)
+    copies[1].wait()
     ks, vs, bias = slot_pair(in_ref)
+    copies[2].wait()
+    copies[3].wait()
     values = jnp.concatenate([vt, vs], axis=0).T
     causal = iota((rows, rows), 0) <= iota((rows, rows), 1)
     for g in range(group):

time: 107 us -> 107 us (level)
  no operation moved by 1% of the time
where the time goes in v6:
time: 107 us; the launch traced here: 106 us
  blocking collectives  55.7 us (52%)
  Pallas kernels  19.4 us (18%)
  waiting for transfers between devices  13.6 us (13%)
  starting transfers between devices  12.4 us (12%)
  local copies, waits for them, and re-layouts  4.31 us (4%)
    all_to_all x2, blocking collectives, exchange(): return lax.all_to_all(x, axes, split_axis=0, concat_axis=0, tiled=True)  42 us
    pallas_call x9, Pallas kernels, call(): pl.pallas_call(kernel, out_shape=out_shape, in_specs=specs or [VM] * len(...  19.4 us
    all_gather x1, blocking collectives, on_device(): x = lax.all_gather(patches.T, 'mp', axis=0, tiled=True)  13.7 us
    all_to_all x3, waiting for transfers between devices, exchange(): return lax.all_to_all(x, axes, split_axis=0, concat_axis=0, tiled=True)  13.6 us
    all_to_all x3, starting transfers between devices, exchange(): return lax.all_to_all(x, axes, split_axis=0, concat_axis=0, tiled=True)  12.4 us
    reshape x1, local copies, waits for them, and re-layouts, on_device(): jnp.transpose(visual_kv.reshape(width, 2, 4, HD), (0, 2, 1, 3))  4.28 us
  transfers between devices with their start and end apart: 3, of which 3 were waited for; matrix products, arithmetic and copies ran while one was open for 4% of the time, Pallas kernels for 7%

profile of v6, /device:TPU:1, one launch (start us, length us, event | category | flops | bytes accessed | tf_op | source)
XLA Modules:
  0.0 106.2 jit_solution(7424060147485184238)
XLA Ops:
  0.6 13.7 %all_gather.3.x_hbm = bf16[1280,256]{1,0:T(8,128)(2,1)} all-gather(bf16[320,256]{1,0:T(8,128)(2,1)} %bitcast.23), channel_id=1, replica_groups=mesh['sec'=2,'dp'=64,'mp'=4] {'mp'}, dimensions={0}, use_global_device_ids=true | all-gather | bytes 819200 | tf_op jit(solution)/shard_map/all_gather | solution.py:320
  14.3 0.0 copy-start.3
  14.3 4.7 %shard_map.131 = (bf16[4,64,1280]{2,1,0:T(8,128)(2,1)}, bf16[64,1280]{1,0:T(8,128)(2,1)}) custom-call(s32[1]{0:T(128)} %bitcast.pos_ref, bf16[10,128]{1,0:T(8,128)(2,1)} %bitcast.27, s32[1,256]{1,0:T(1,128)} %bitcast.28, bf16[480,1280]{1,0:T(8,128)(2,1)} %bitcast.24, bf16[1280,256]{1,0:T(8,128)(2,1)} %all_gather.3.x_hbm, bf16[160,1280]{1,0:T(8,128)(2,1)} %proj_hbm.1), custom_call_target="tpu_custom_call" | custom-call | flops 1000000000 | bytes 4000000 | tf_op jit(solution)/shard_map/pallas_call | solution.py:37
  19.0 3.5 %all-to-all-start = ((bf16[4,64,1280]{2,1,0:T(8,128)(2,1)}), bf16[4,64,1280]{2,1,0:T(8,128)(2,1)S(1)}, u32[]{:S(2)}, u32[]{:S(2)}) async-start(bf16[4,64,1280]{2,1,0:T(8,128)(2,1)} %get-tuple-element.11), calls=%async_computation | async-start | bytes 1310720 | tf_op jit(solution)/shard_map/all_to_all | solution.py:304
  22.5 0.0 copy-done.3
  22.6 0.0 copy-start
  22.6 4.3 %reshape.52.w_ref = bf16[1280,1024]{1,0:T(8,128)(2,1)S(1)} reshape(bf16[1280,4,2,128]{3,2,1,0:T(2,128)(2,1)} %bitcast.22) | data formatting | bytes 5242880 | tf_op jit(solution)/shard_map/reshape | solution.py:337
  26.9 0.0 copy-start.1
  26.9 0.0 copy-start.2
  26.9 3.3 %all-to-all-done.in_ref = bf16[4,64,1280]{2,1,0:T(8,128)(2,1)S(1)} async-done(((bf16[4,64,1280]{2,1,0:T(8,128)(2,1)}), bf16[4,64,1280]{2,1,0:T(8,128)(2,1)S(1)}, u32[]{:S(2)}, u32[]{:S(2)}) %all-to-all-start) | async-done | bytes 655392 | tf_op jit(solution)/shard_map/all_to_all | solution.py:304
  30.1 0.0 copy-done
  30.1 1.4 %shard_map.132 = bf16[4,64,256]{2,1,0:T(8,128)(2,1)} custom-call(bf16[4,64,1280]{2,1,0:T(8,128)(2,1)S(1)} %all-to-all-done.in_ref, bf16[64,1280]{1,0:T(8,128)(2,1)S(1)} %copy-done, bf16[1,1280]{1,0:T(2,128)(2,1)S(1)} %reshape.50.gain_ref, bf16[1280,1024]{1,0:T(8,128)(2,1)S(1)} %reshape.52.w_ref), custom_call_target="tpu_custom_call" | custom-call | flops 200000000 | bytes 4000000 | tf_op jit(solution)/shard_map/pallas_call | solution.py:37
  31.5 3.3 %all-to-all-start.1 = ((bf16[4,64,256]{2,1,0:T(8,128)(2,1)}), bf16[4,64,256]{2,1,0:T(8,128)(2,1)S(1)}, u32[]{:S(2)}, u32[]{:S(2)}) async-start(bf16[4,64,256]{2,1,0:T(8,128)(2,1)} %shard_map.132), calls=%async_computation.1 | async-start | bytes 262144 | tf_op jit(solution)/shard_map/all_to_all | solution.py:304
  34.9 0.0 copy-done.1
  34.9 0.0 copy-done.2
  34.9 0.1 shard_map.134.code_hbm.code_ref
  35.0 2.8 %shard_map.133.text_hbm = f32[1024,256]{1,0:T(8,128)} custom-call(bf16[512,128]{1,0:T(8,128)(2,1)} %bitcast.25, bf16[256,1024]{1,0:T(8,128)(2,1)} %q_hbm.5, bf16[256,1024]{1,0:T(8,128)(2,1)} %c_hbm.3), custom_call_target="tpu_custom_call" | custom-call | flops 1000000000 | bytes 2000000 | tf_op jit(solution)/shard_map/pallas_call | solution.py:37
  37.8 1.9 %all-to-all-done.1.in_ref = bf16[4,64,256]{2,1,0:T(8,128)(2,1)S(1)} async-done(((bf16[4,64,256]{2,1,0:T(8,128)(2,1)}), bf16[4,64,256]{2,1,0:T(8,128)(2,1)S(1)}, u32[]{:S(2)}, u32[]{:S(2)}) %all-to-all-start.1) | async-done | bytes 131104 | tf_op jit(solution)/shard_map/all_to_all | solution.py:304
  39.7 0.2 shard_map.135
  39.9 34.8 %all_to_all.25 = bf16[128,4,128]{2,1,0:T(4,128)(2,1)S(1)} all-to-all(bf16[128,4,128]{2,1,0:T(4,128)(2,1)S(1)} %bitcast.18), channel_id=1, replica_groups=mesh['sec'=2,'dp'=64,'mp'=4] {'dp','sec'}, dimensions={0} | all-to-all | bytes 262144 | tf_op jit(solution)/shard_map/all_to_all | solution.py:304
  74.7 4.0 %shard_map.136 = (bf16[512,128]{1,0:T(8,128)(2,1)}, f32[1024,256]{1,0:T(8,128)}, bf16[4096,128]{1,0:T(8,128)(2,1)}) custom-call(bf16[512,128]{1,0:T(8,128)(2,1)S(1)} %bitcast.19, f32[1024,256]{1,0:T(8,128)} %shard_map.133.text_hbm, bf16[256,1024]{1,0:T(8,128)(2,1)} %q_hbm.5, bf16[256,1024]{1,0:T(8,128)(2,1)} %c_hbm.3), custom_call_target="tpu_custom_call" | custom-call | flops 1000000000 | bytes 2000000 | tf_op jit(solution)/shard_map/pallas_call | solution.py:37
  78.7 5.6 %all-to-all-start.3 = ((bf16[128,4,128]{2,1,0:T(4,128)(2,1)}), bf16[128,4,128]{2,1,0:T(4,128)(2,1)S(1)}, u32[]{:S(2)}, u32[]{:S(2)}) async-start(bf16[128,4,128]{2,1,0:T(4,128)(2,1)} %bitcast.13), calls=%async_computation.3 | async-start | bytes 262144 | tf_op jit(solution)/shard_map/all_to_all | solution.py:304
  84.3 4.3 %shard_map.137 = bf16[256,1024]{1,0:T(8,128)(2,1)} custom-call(bf16[4096,128]{1,0:T(8,128)(2,1)} %get-tuple-element.16.in_hbm, bf16[512,128]{1,0:T(8,128)(2,1)} %bitcast.26, f32[1024,256]{1,0:T(8,128)} %get-tuple-element.17.stats_hbm, bf16[256,1024]{1,0:T(8,128)(2,1)} %q_hbm.5), custom_call_target="tpu_custom_call" | custom-call | flops 1000000000 | bytes 2000000 | tf_op jit(solution)/shard_map/pallas_call | solution.py:37
  88.6 8.5 %all-to-all-done.3 = bf16[128,4,128]{2,1,0:T(4,128)(2,1)S(1)} async-done(((bf16[128,4,128]{2,1,0:T(4,128)(2,1)}), bf16[128,4,128]{2,1,0:T(4,128)(2,1)S(1)}, u32[]{:S(2)}, u32[]{:S(2)}) %all-to-all-start.3) | async-done | bytes 131104 | tf_op jit(solution)/shard_map/all_to_all | solution.py:304
  97.1 0.3 shard_map.138
  97.4 7.2 %all_to_all.26.in_ref = bf16[4,64,256]{2,1,0:T(8,128)(2,1)S(1)} all-to-all(bf16[4,64,256]{2,1,0:T(8,128)(2,1)S(1)} %shard_map.138), channel_id=1, replica_groups=mesh['sec'=2,'dp'=64,'mp'=4] {'mp'}, dimensions={0} | all-to-all | bytes 262144 | tf_op jit(solution)/shard_map/all_to_all | solution.py:304
  104.7 1.5 %shard_map.139 = bf16[64,1280]{1,0:T(8,128)(2,1)} custom-call(bf16[4,64,256]{2,1,0:T(8,128)(2,1)S(1)} %all_to_all.26.in_ref, bf16[1280,1024]{1,0:T(8,128)(2,1)S(1)} %reshape.52.w_ref), custom_call_target="tpu_custom_call" | custom-call | flops 200000000 | bytes 3000000 | tf_op jit(solution)/shard_map/pallas_call | solution.py:37
  (1 shorter events, 0.0 us)
Async XLA Ops:
  14.3 8.2 %copy-start.3 = (bf16[1280]{0:T(1024)(128)(2,1)S(1)}, bf16[1280]{0:T(1024)(128)(2,1)}, u32[]{:S(2)}) copy-start(bf16[1280]{0:T(1024)(128)(2,1)} %param.17) | copy-start | bytes 7684
  19.0 11.1 %all-to-all-start = ((bf16[4,64,1280]{2,1,0:T(8,128)(2,1)}), bf16[4,64,1280]{2,1,0:T(8,128)(2,1)S(1)}, u32[]{:S(2)}, u32[]{:S(2)}) async-start(bf16[4,64,1280]{2,1,0:T(8,128)(2,1)} %get-tuple-element.11), calls=%async_computation | async-start | bytes 1310720 | tf_op jit(solution)/shard_map/all_to_all | solution.py:304
  22.6 7.6 %copy-start = (bf16[64,1280]{1,0:T(8,128)(2,1)S(1)}, bf16[64,1280]{1,0:T(8,128)(2,1)}, u32[]{:S(2)}) copy-start(bf16[64,1280]{1,0:T(8,128)(2,1)} %get-tuple-element.12.own_ref) | copy-start | bytes 491524
  26.9 8.0 %copy-start.1 = (s32[64]{0:T(128)S(1)}, s32[64]{0:T(128)}, u32[]{:S(2)}) copy-start(s32[64]{0:T(128)} %param.18) | copy-start | bytes 772
  26.9 8.0 %copy-start.2 = (s32[64]{0:T(128)S(1)}, s32[64]{0:T(128)}, u32[]{:S(2)}) copy-start(s32[64]{0:T(128)} %param.19) | copy-start | bytes 772
  31.5 8.1 %all-to-all-start.1 = ((bf16[4,64,256]{2,1,0:T(8,128)(2,1)}), bf16[4,64,256]{2,1,0:T(8,128)(2,1)S(1)}, u32[]{:S(2)}, u32[]{:S(2)}) async-start(bf16[4,64,256]{2,1,0:T(8,128)(2,1)} %shard_map.132), calls=%async_computation.1 | async-start | bytes 262144 | tf_op jit(solution)/shard_map/all_to_all | solution.py:304
  78.7 18.4 %all-to-all-start.3 = ((bf16[128,4,128]{2,1,0:T(4,128)(2,1)}), bf16[128,4,128]{2,1,0:T(4,128)(2,1)S(1)}, u32[]{:S(2)}, u32[]{:S(2)}) async-start(bf16[128,4,128]{2,1,0:T(4,128)(2,1)} %bitcast.13), calls=%async_computation.3 | async-start | bytes 262144 | tf_op jit(solution)/shard_map/all_to_all | solution.py:304
